TPU v7x, 512 devices: a whole 4x4x16 slice. The times are simulated.
512 devices in a mesh: gx: 8 (over y, z_hi), gy: 16 (over z_lo, core), frame: 4 (over x).
Axes of the slice: x: 4, y: 4, z: 16 (z_hi: 2, z_lo: 8; z = z_hi * 8 + z_lo), core: 2. Of those that a mesh axis runs over, the one named last changes fastest.
Arguments:
- features: bfloat16 [32, 32, 128, 128], P(('frame', 'gx'), 'gy'), parts along dimension 0, may hold values from -6 to 6
- positions: float32 [32, 32, 3, 128], P(('frame', 'gx'), 'gy'), parts along dimension 0, may hold values from 0 to 1
- bead_types: int32 [32, 32, 128], P(('frame', 'gx'), 'gy'), parts along dimension 0, may hold values from 0 to 15
- cell_counts: int32 [32, 32], P(('frame', 'gx'), 'gy'), parts along dimension 0, may hold values from 48 to 128
- w_value: bfloat16 [128, 128], replicated, may hold values from -0.5 to 0.5
- w_radial: float32 [8, 128], replicated, may hold values from -0.6 to 0.6
- type_gain: float32 [16, 128], replicated, may hold values from 0.1 to 1.9
- w_out: bfloat16 [128, 128], replicated, may hold values from -0.5 to 0.5
- cotangent: bfloat16 [32, 32, 128, 128], P(('frame', 'gx'), 'gy'), parts along dimension 0, may hold values from -6 to 6
Outputs:
- out_feat: bfloat16 [32, 32, 128, 128], P(('frame', 'gx'), 'gy'), parts along dimension 0
- grad_feat: bfloat16 [32, 32, 128, 128], P(('frame', 'gx'), 'gy'), parts along dimension 0
- grad_pos: float32 [32, 32, 3, 128], P(('frame', 'gx'), 'gy'), parts along dimension 0
- grad_wvalue: float32 [512, 128], P('frame'), parts along dimension 0
- grad_wradial: float32 [32, 128], P('frame'), parts along dimension 0
- grad_gain: float32 [64, 128], P('frame'), parts along dimension 0
- grad_wout: float32 [512, 128], P('frame'), parts along dimension 0
There are 4 independent parts, one for each index of `frame`. A program takes and returns all parts, laid end to end along the dimension named above; an argument that names none is the same for every part. Nothing has to cross between parts.
All inputs are finite; a program needn't handle non-finite values.
Results may differ from a plain program's by a relative error of at most 0.012.
Values may be sent and summed in bfloat16 or wider, within the bound.
A program may use at most 64 MiB of HBM per device.

v0:
```python
import jax
import jax.numpy as jnp
from jax import lax
from jax.sharding import PartitionSpec as P

HZ = 6


soften = 0.01
stencil = [(-1, -1), (-1, 0), (-1, 1), (0, -1), (0, 0), (0, 1), (1, -1), (1, 0), (1, 1)]


def passed_along(block, axis, distance):
    devices = range(lax.axis_size(axis))
    route = [((i - distance) % len(devices), i) for i in devices]
    return lax.ppermute(block, axis, route)


def with_halo(block, sides, width):
    for axis, dim in sides:
        count = lax.axis_size(axis)
        forward = [(i, i + 1) for i in range(count - 1)]
        forward.append((count - 1, 0))
        backward = [(target, source) for source, target in forward]
        low = lax.ppermute(
            lax.slice_in_dim(block, block.shape[dim] - width, None, axis=dim), axis, forward
        )
        high = lax.ppermute(lax.slice_in_dim(block, 0, width, axis=dim), axis, backward)
        block = jnp.concatenate([low, block, high], axis=dim)
    return block


def pair_terms(pos_own, pos_near, shift_x, shift_y, is_self, basis_count):
    slot_count = pos_own.shape[-1]
    offsets = (float(shift_x), float(shift_y), 0.0)
    scales = (1.0, 1.0, float(HZ))
    deltas = [
        (pos_near[:, :, component, None, :] - pos_own[:, :, component, :, None]) * scales[component]
        + offsets[component]
        for component in range(3)
    ]
    dist_sq = deltas[0] * deltas[0] + deltas[1] * deltas[1] + deltas[2] * deltas[2]
    pair_mask = pos_own[:, :, 3, :, None] * pos_near[:, :, 3, None, :]
    if is_self:
        pair_mask = pair_mask * (1.0 - jnp.eye(slot_count, dtype=jnp.float32))
    radius = jnp.sqrt(dist_sq + soften)
    inside = jnp.maximum(1.0 - dist_sq, 0.0)
    envelope = inside * inside
    centres = jnp.arange(basis_count, dtype=jnp.float32) / (basis_count - 1)
    width_gamma = 0.5 * (basis_count - 1) ** 2
    offset_r = radius[:, :, None] - centres[None, None, :, None, None]
    gaussian = jnp.exp(-width_gamma * offset_r * offset_r)
    weights = ((pair_mask * envelope)[:, :, None] * gaussian).astype(jnp.bfloat16)
    slope_r2 = (
        pair_mask[:, :, None]
        * gaussian
        * (
            -2.0 * inside[:, :, None]
            - envelope[:, :, None] * width_gamma * offset_r / radius[:, :, None]
        )
    )
    scaled_deltas = [deltas[component] * scales[component] for component in range(3)]
    return (weights, slope_r2, scaled_deltas)


def fold_back(pos_accum, val_accum):
    row_count = pos_accum.shape[0] - 2
    for step_by, source, target in ((1, row_count + 1, 1), (-1, 0, row_count)):
        received = passed_along((pos_accum[source], val_accum[source]), "gx", step_by)
        pos_accum = pos_accum.at[target].add(received[0])
        val_accum = val_accum.at[target].add(received[1])
    pos_accum = pos_accum[1 : row_count + 1]
    val_accum = val_accum[1 : row_count + 1]
    col_count = pos_accum.shape[1] - 2
    for step_by, source, target in ((1, col_count + 1, 1), (-1, 0, col_count)):
        received = passed_along((pos_accum[:, source], val_accum[:, source]), "gy", step_by)
        pos_accum = pos_accum.at[:, target].add(received[0])
        val_accum = val_accum.at[:, target].add(received[1])
    return (pos_accum[:, 1 : col_count + 1], val_accum[:, 1 : col_count + 1])


def on_device(
    features, positions, bead_types, cell_counts, w_value, w_radial, type_gain, w_out, cotangent
):
    row_count, col_count, slot_count, channels = features.shape
    basis_count = w_radial.shape[0]
    valid_slot = (
        jnp.arange(slot_count, dtype=jnp.int32)[None, None, :] < cell_counts[:, :, None]
    ).astype(jnp.float32)
    pos_valid = jnp.concatenate([positions, valid_slot[:, :, None, :]], axis=2)
    flat_feat = features.reshape(-1, channels)
    projected = jnp.dot(flat_feat, w_value, preferred_element_type=jnp.float32)
    onehot = (
        bead_types.reshape(-1)[:, None] == jnp.arange(type_gain.shape[0], dtype=jnp.int32)[None, :]
    ).astype(jnp.float32)
    bead_gain = jnp.dot(onehot, type_gain, precision=lax.Precision.HIGHEST)
    carried = (
        (projected * bead_gain)
        .astype(jnp.bfloat16)
        .reshape(row_count, col_count, slot_count, channels)
    )
    pos_ext = with_halo(pos_valid, (("gx", 0), ("gy", 1)), 1)
    val_ext = with_halo(carried, (("gx", 0), ("gy", 1)), 1)

    def near_cells(extended, shift_x, shift_y):
        return extended[
            1 + shift_x : 1 + shift_x + row_count, 1 + shift_y : 1 + shift_y + col_count
        ]

    summed = jnp.zeros((row_count, col_count, basis_count, slot_count, channels), jnp.float32)
    for shift_x, shift_y in stencil:
        weights, slope_r2, deltas = pair_terms(
            pos_valid,
            near_cells(pos_ext, shift_x, shift_y),
            shift_x,
            shift_y,
            shift_x == 0 and shift_y == 0,
            basis_count,
        )
        summed = summed + jnp.einsum(
            "abkij,abjc->abkic",
            weights,
            near_cells(val_ext, shift_x, shift_y),
            preferred_element_type=jnp.float32,
        )
    aggregate = jnp.sum(summed * w_radial[None, None, :, None, :], axis=2)
    agg_half = aggregate.astype(jnp.bfloat16).reshape(-1, channels)
    pre_act = jnp.dot(agg_half, w_out, preferred_element_type=jnp.float32)
    sigmoid_act = jax.nn.sigmoid(pre_act)
    out_feat = (flat_feat.astype(jnp.float32) + pre_act * sigmoid_act).astype(jnp.bfloat16)
    grad_pre = (
        cotangent.reshape(-1, channels).astype(jnp.float32)
        * sigmoid_act
        * (1.0 + pre_act * (1.0 - sigmoid_act))
    ).astype(jnp.bfloat16)
    grad_wout = jnp.dot(agg_half.T, grad_pre, preferred_element_type=jnp.float32)
    grad_agg = (
        jnp.dot(grad_pre, w_out.T, preferred_element_type=jnp.float32)
        .astype(jnp.bfloat16)
        .reshape(row_count, col_count, slot_count, channels)
    )
    grad_wradial = jnp.sum(summed * grad_agg.astype(jnp.float32)[:, :, None], axis=(0, 1, 3))
    scaled = (grad_agg.astype(jnp.float32)[:, :, None] * w_radial[None, None, :, None, :]).astype(
        jnp.bfloat16
    )
    pos_accum = jnp.zeros((row_count + 2, col_count + 2, 3, slot_count), jnp.float32)
    val_accum = jnp.zeros((row_count + 2, col_count + 2, slot_count, channels), jnp.float32)
    for shift_x, shift_y in stencil:
        weights, slope_r2, deltas = pair_terms(
            pos_valid,
            near_cells(pos_ext, shift_x, shift_y),
            shift_x,
            shift_y,
            shift_x == 0 and shift_y == 0,
            basis_count,
        )
        weight_grad = jnp.einsum(
            "abkic,abjc->abkij",
            scaled,
            near_cells(val_ext, shift_x, shift_y),
            preferred_element_type=jnp.float32,
        )
        pair_pull = jnp.sum(weight_grad * slope_r2, axis=2)
        own_pull = jnp.stack(
            [-2.0 * jnp.sum(pair_pull * delta_one, axis=3) for delta_one in deltas], axis=2
        )
        far_pull = jnp.stack(
            [2.0 * jnp.sum(pair_pull * delta_one, axis=2) for delta_one in deltas], axis=2
        )
        far_value = jnp.einsum(
            "abkij,abkic->abjc", weights, scaled, preferred_element_type=jnp.float32
        )
        pos_accum = pos_accum.at[1 : row_count + 1, 1 : col_count + 1].add(own_pull)
        pos_accum = pos_accum.at[
            1 + shift_x : 1 + shift_x + row_count, 1 + shift_y : 1 + shift_y + col_count
        ].add(far_pull)
        val_accum = val_accum.at[
            1 + shift_x : 1 + shift_x + row_count, 1 + shift_y : 1 + shift_y + col_count
        ].add(far_value)
    grad_pos, grad_carried = fold_back(pos_accum, val_accum)
    flat_carried = grad_carried.reshape(-1, channels)
    grad_half = (flat_carried * bead_gain).astype(jnp.bfloat16)
    grad_feat = (
        cotangent.reshape(-1, channels).astype(jnp.float32)
        + jnp.dot(grad_half, w_value.T, preferred_element_type=jnp.float32)
    ).astype(jnp.bfloat16)
    grad_wvalue = jnp.dot(flat_feat.T, grad_half, preferred_element_type=jnp.float32)
    grad_gain = jnp.dot(onehot.T, flat_carried * projected, precision=lax.Precision.HIGHEST)
    summed_grads = lax.psum((grad_wvalue, grad_wradial, grad_gain, grad_wout), ("gx", "gy"))
    return (
        out_feat.reshape(row_count, col_count, slot_count, channels),
        grad_feat.reshape(row_count, col_count, slot_count, channels),
        grad_pos,
        summed_grads[0],
        summed_grads[1],
        summed_grads[2],
        summed_grads[3],
    )


def solution(mesh):
    return jax.shard_map(
        on_device,
        mesh=mesh,
        in_specs=(
            P(("frame", "gx"), "gy", None, None),
            P(("frame", "gx"), "gy", None, None),
            P(("frame", "gx"), "gy", None),
            P(("frame", "gx"), "gy"),
            P(),
            P(),
            P(),
            P(),
            P(("frame", "gx"), "gy", None, None),
        ),
        out_specs=(
            P(("frame", "gx"), "gy", None, None),
            P(("frame", "gx"), "gy", None, None),
            P(("frame", "gx"), "gy", None, None),
            P("frame", None),
            P("frame", None),
            P("frame", None),
            P("frame", None),
        ),
        check_vma=False,
    )
```

profile of v0, /device:TPU:1, one launch (start us, length us, event | category | flops | bytes accessed | tf_op | source)
XLA Modules:
  0.0 693.5 jit_solution(3987347894416021543)
XLA Ops:
  7.3 0.6 copy-done.12
  7.9 16.3 %collective-permute-start = (f32[1,2,4,128]{3,1,2,0:T(2,128)S(1)}, f32[1,2,4,128]{3,1,2,0:T(2,128)S(1)}, u32[]{:S(2)}, u32[]{:S(2)}) collective-permute-start(f32[1,2,4,128]{3,1,2,0:T(2,128)S(1)} %pad_maximum_fusion.8), channel_id=1, source_target_pairs={{0,64},{64,128},{128,192},{192,256},{256,320},{320,384},{384,448},... | collective-permute-start | bytes 12296 | tf_op jit(solution)/shard_map/ppermute | solution.py:25
  24.2 4.4 collective-permute-start.1
  29.6 9.6 %collective-permute-start.3 = (bf16[1,2,128,128]{3,2,1,0:T(8,128)(2,1)S(1)}, bf16[1,2,128,128]{3,2,1,0:T(8,128)(2,1)S(1)}, u32[]{:S(2)}, u32[]{:S(2)}) collective-permute-start(bf16[1,2,128,128]{3,2,1,0:T(8,128)(2,1)S(1)} %bitcast.388), channel_id=1, source_target_pairs={{0,64},{64,128},{128,192},{192,256},{256,320},{320,384},{384,448},... | collective-permute-start | bytes 196616 | tf_op jit(solution)/shard_map/ppermute | solution.py:25
  39.2 6.5 collective-permute-start.4
  46.5 0.7 and_reduce_fusion
  47.8 4.0 collective-permute-start.2
  51.9 3.2 collective-permute-start.6
  55.2 1.6 collective-permute-done.6
  58.8 2.0 collective-permute-start.5
  60.8 10.0 %collective-permute-start.7 = (bf16[3,1,128,128]{3,2,1,0:T(8,128)(2,1)S(1)}, bf16[3,1,128,128]{3,2,1,0:T(8,128)(2,1)S(1)}, u32[]{:S(2)}, u32[]{:S(2)}) collective-permute-start(bf16[3,1,128,128]{3,2,1,0:T(8,128)(2,1)S(1)} %get-tuple-element.583), channel_id=1, source_target_pairs={{4,0},{8,4},{12,8},{16,12},{20,16},{24,20},{28,24},{32,28},{36,32}... | collective-permute-start | bytes 294920 | tf_op jit(solution)/shard_map/ppermute | solution.py:28
  73.5 0.6 fusion.5
  74.1 0.7 copy-done.9
  74.8 0.6 multiply_reduce_fusion.1
  75.6 0.8 fusion.159
  77.3 1.8 fusion.16
  79.1 2.5 fusion.19
  84.8 0.6 fusion.8
  85.8 0.6 fusion.9
  86.4 0.6 fusion.10
  87.1 0.6 fusion.11
  87.7 0.6 fusion.7
  88.3 0.7 fusion.223
  89.1 0.6 fusion.12
  89.7 0.8 fusion.14
  90.6 0.6 fusion.6
  91.2 0.6 fusion.13
  91.8 0.7 fusion.219
  92.8 1.3 fusion.280
  94.1 1.4 scatter-add.126
  95.7 2.0 add_select_fusion
  97.7 1.4 scatter-add.130
  100.6 5.9 collective-permute-start.12
  106.4 10.3 %collective-permute-start.13 = (f32[4,3,128]{2,0,1:T(4,128)S(1)}, f32[4,3,128]{2,0,1:T(4,128)S(1)}, u32[]{:S(2)}, u32[]{:S(2)}) collective-permute-start(f32[4,3,128]{2,0,1:T(4,128)S(1)} %get-tuple-element.591), channel_id=1, source_target_pairs={{64,0},{128,64},{192,128},{256,192},{320,256},{384,320},{448,384},... | collective-permute-start | bytes 18440 | tf_op jit(solution)/shard_map/ppermute | solution.py:16
  116.7 0.8 fusion.305
  117.5 3.7 collective-permute-start.8
  121.3 12.4 %collective-permute-start.9 = (f32[4,128,128]{2,1,0:T(8,128)S(1)}, f32[4,128,128]{2,1,0:T(8,128)S(1)}, u32[]{:S(2)}, u32[]{:S(2)}) collective-permute-start(f32[4,128,128]{2,1,0:T(8,128)S(1)} %get-tuple-element.575), channel_id=1, source_target_pairs={{64,0},{128,64},{192,128},{256,192},{320,256},{384,320},{448,384},... | collective-permute-start | bytes 786440 | tf_op jit(solution)/shard_map/ppermute | solution.py:16
  133.7 1.9 collective-permute-start.14
  135.7 30.2 %collective-permute-done.14 = f32[1,3,128]{2,0,1:T(1,128)S(1)} collective-permute-done((f32[1,3,128]{2,0,1:T(1,128)S(1)}, f32[1,3,128]{2,0,1:T(1,128)S(1)}, u32[]{:S(2)}, u32[]{:S(2)}) %collective-permute-start.14) | collective-permute-done | bytes 1568 | tf_op jit(solution)/shard_map/ppermute | solution.py:16
  166.0 4.1 collective-permute-done.9
  170.1 1.9 collective-permute-start.10
  172.0 3.5 collective-permute-start.15
  175.6 10.2 %collective-permute-start.11 = (f32[1,128,128]{2,1,0:T(8,128)S(1)}, f32[1,128,128]{2,1,0:T(8,128)S(1)}, u32[]{:S(2)}, u32[]{:S(2)}) collective-permute-start(f32[1,128,128]{2,1,0:T(8,128)S(1)} %slice_bitcast_fusion.2), channel_id=1, source_target_pairs={{4,0},{8,4},{12,8},{16,12},{20,16},{24,20},{28,24},{32,28},{36,32}... | collective-permute-start | bytes 196616 | tf_op jit(solution)/shard_map/ppermute | solution.py:16
  186.8 0.8 convolution_bitcast_fusion.9
  187.7 0.8 fusion.32
  188.8 495.6 %all-reduce.2 = (f32[8,128]{1,0:T(8,128)}, f32[16,128]{1,0:T(8,128)}) all-reduce(f32[8,128]{1,0:T(8,128)S(1)} %multiply_reduce_fusion, f32[16,128]{1,0:T(8,128)S(1)} %fusion.203), channel_id=1, replica_groups=mesh['gx'=8,'gy'=16,'frame'=4] {'gx','gy'}, use_global_device_ids=true, to_apply=%region_67.0 | all-reduce | flops 3072 | bytes 24576 | tf_op jit(solution)/shard_map/psum | solution.py:189
  684.4 1.6 copy.44
  686.0 0.6 copy.105
  (155 shorter events, 14.6 us)
Async XLA Ops:
  7.2 68.2 %copy-start = (bf16[128,128]{1,0:T(8,128)(2,1)S(1)}, bf16[128,128]{1,0:T(8,128)(2,1)}, u32[]{:S(2)}) copy-start(bf16[128,128]{1,0:T(8,128)(2,1)} %param.86) | copy-start | bytes 98308
  7.2 0.7 copy-start.12
  7.2 0.7 copy-start.1
  7.2 21.4 %copy-start.8 = (f32[16,128]{1,0:T(8,128)S(1)}, f32[16,128]{1,0:T(8,128)}, u32[]{:S(2)}) copy-start(f32[16,128]{1,0:T(8,128)} %param.85) | copy-start | bytes 24580
  7.2 677.2 %all-reduce.6.cloned.1.call-start = ((), (), s32[]{:S(2)}) async-start(), calls=%async_computation | async-start | bytes 262144 | tf_op jit(solution)/shard_map/psum | solution.py:189
  7.9 20.7 %copy-start.10 = (s32[1,2,128]{2,1,0:T(2,128)S(1)}, s32[1,2,128]{2,1,0:T(2,128)}, u32[]{:S(2)}) copy-start(s32[1,2,128]{2,1,0:T(2,128)} %param.81) | copy-start | bytes 3076
  7.9 39.9 %collective-permute-start = (f32[1,2,4,128]{3,1,2,0:T(2,128)S(1)}, f32[1,2,4,128]{3,1,2,0:T(2,128)S(1)}, u32[]{:S(2)}, u32[]{:S(2)}) collective-permute-start(f32[1,2,4,128]{3,1,2,0:T(2,128)S(1)} %pad_maximum_fusion.8), channel_id=1, source_target_pairs={{0,64},{64,128},{128,192},{192,256},{256,320},{320,384},{384,448},... | collective-permute-start | bytes 12296 | tf_op jit(solution)/shard_map/ppermute | solution.py:25
  24.2 23.6 %collective-permute-start.1 = (f32[1,2,4,128]{3,1,2,0:T(2,128)S(1)}, f32[1,2,4,128]{3,1,2,0:T(2,128)S(1)}, u32[]{:S(2)}, u32[]{:S(2)}) collective-permute-start(f32[1,2,4,128]{3,1,2,0:T(2,128)S(1)} %pad_maximum_fusion.8), channel_id=1, source_target_pairs={{64,0},{128,64},{192,128},{256,192},{320,256},{384,320},{448,384},... | collective-permute-start | bytes 12296 | tf_op jit(solution)/shard_map/ppermute | solution.py:28
  28.6 0.8 copy-start.2
  28.6 0.8 copy-start.3
  29.6 29.2 %collective-permute-start.3 = (bf16[1,2,128,128]{3,2,1,0:T(8,128)(2,1)S(1)}, bf16[1,2,128,128]{3,2,1,0:T(8,128)(2,1)S(1)}, u32[]{:S(2)}, u32[]{:S(2)}) collective-permute-start(bf16[1,2,128,128]{3,2,1,0:T(8,128)(2,1)S(1)} %bitcast.388), channel_id=1, source_target_pairs={{0,64},{64,128},{128,192},{192,256},{256,320},{320,384},{384,448},... | collective-permute-start | bytes 196616 | tf_op jit(solution)/shard_map/ppermute | solution.py:25
  39.2 19.5 %collective-permute-start.4 = (bf16[1,2,128,128]{3,2,1,0:T(8,128)(2,1)S(1)}, bf16[1,2,128,128]{3,2,1,0:T(8,128)(2,1)S(1)}, u32[]{:S(2)}, u32[]{:S(2)}) collective-permute-start(bf16[1,2,128,128]{3,2,1,0:T(8,128)(2,1)S(1)} %bitcast.389), channel_id=1, source_target_pairs={{64,0},{128,64},{192,128},{256,192},{320,256},{384,320},{448,384},... | collective-permute-start | bytes 196616 | tf_op jit(solution)/shard_map/ppermute | solution.py:28
  45.8 0.7 copy-start.11
  47.8 7.3 %collective-permute-start.2 = (f32[3,1,4,128]{3,1,2,0:T(1,128)S(1)}, f32[3,1,4,128]{3,1,2,0:T(1,128)S(1)}, u32[]{:S(2)}, u32[]{:S(2)}) collective-permute-start(f32[3,1,4,128]{3,1,2,0:T(1,128)S(1)} %get-tuple-element.616), channel_id=1, source_target_pairs={{0,4},{4,8},{8,12},{12,16},{16,20},{20,24},{24,28},{28,32},{32,36}... | collective-permute-start | bytes 18440 | tf_op jit(solution)/shard_map/ppermute | solution.py:25
  51.9 4.9 collective-permute-start.6
  58.8 12.8 %collective-permute-start.5 = (bf16[3,1,128,128]{3,2,1,0:T(8,128)(2,1)S(1)}, bf16[3,1,128,128]{3,2,1,0:T(8,128)(2,1)S(1)}, u32[]{:S(2)}, u32[]{:S(2)}) collective-permute-start(bf16[3,1,128,128]{3,2,1,0:T(8,128)(2,1)S(1)} %get-tuple-element.582), channel_id=1, source_target_pairs={{0,4},{4,8},{8,12},{12,16},{16,20},{20,24},{24,28},{28,32},{32,36}... | collective-permute-start | bytes 294920 | tf_op jit(solution)/shard_map/ppermute | solution.py:25
  60.8 11.4 %collective-permute-start.7 = (bf16[3,1,128,128]{3,2,1,0:T(8,128)(2,1)S(1)}, bf16[3,1,128,128]{3,2,1,0:T(8,128)(2,1)S(1)}, u32[]{:S(2)}, u32[]{:S(2)}) collective-permute-start(bf16[3,1,128,128]{3,2,1,0:T(8,128)(2,1)S(1)} %get-tuple-element.583), channel_id=1, source_target_pairs={{4,0},{8,4},{12,8},{16,12},{20,16},{24,20},{28,24},{32,28},{36,32}... | collective-permute-start | bytes 294920 | tf_op jit(solution)/shard_map/ppermute | solution.py:28
  74.1 0.7 copy-start.9
  74.8 0.8 copy-start.5
  100.6 33.1 %collective-permute-start.12 = (f32[4,3,128]{2,0,1:T(4,128)S(1)}, f32[4,3,128]{2,0,1:T(4,128)S(1)}, u32[]{:S(2)}, u32[]{:S(2)}) collective-permute-start(f32[4,3,128]{2,0,1:T(4,128)S(1)} %get-tuple-element.590), channel_id=1, source_target_pairs={{448,0},{0,64},{64,128},{128,192},{192,256},{256,320},{320,384},{3... | collective-permute-start | bytes 18440 | tf_op jit(solution)/shard_map/ppermute | solution.py:16
  106.4 27.2 %collective-permute-start.13 = (f32[4,3,128]{2,0,1:T(4,128)S(1)}, f32[4,3,128]{2,0,1:T(4,128)S(1)}, u32[]{:S(2)}, u32[]{:S(2)}) collective-permute-start(f32[4,3,128]{2,0,1:T(4,128)S(1)} %get-tuple-element.591), channel_id=1, source_target_pairs={{64,0},{128,64},{192,128},{256,192},{320,256},{384,320},{448,384},... | collective-permute-start | bytes 18440 | tf_op jit(solution)/shard_map/ppermute | solution.py:16
  117.5 48.4 %collective-permute-start.8 = (f32[4,128,128]{2,1,0:T(8,128)S(1)}, f32[4,128,128]{2,1,0:T(8,128)S(1)}, u32[]{:S(2)}, u32[]{:S(2)}) collective-permute-start(f32[4,128,128]{2,1,0:T(8,128)S(1)} %get-tuple-element.574), channel_id=1, source_target_pairs={{448,0},{0,64},{64,128},{128,192},{192,256},{256,320},{320,384},{3... | collective-permute-start | bytes 786440 | tf_op jit(solution)/shard_map/ppermute | solution.py:16
  121.3 48.8 %collective-permute-start.9 = (f32[4,128,128]{2,1,0:T(8,128)S(1)}, f32[4,128,128]{2,1,0:T(8,128)S(1)}, u32[]{:S(2)}, u32[]{:S(2)}) collective-permute-start(f32[4,128,128]{2,1,0:T(8,128)S(1)} %get-tuple-element.575), channel_id=1, source_target_pairs={{64,0},{128,64},{192,128},{256,192},{320,256},{384,320},{448,384},... | collective-permute-start | bytes 786440 | tf_op jit(solution)/shard_map/ppermute | solution.py:16
  133.7 32.2 %collective-permute-start.14 = (f32[1,3,128]{2,0,1:T(1,128)S(1)}, f32[1,3,128]{2,0,1:T(1,128)S(1)}, u32[]{:S(2)}, u32[]{:S(2)}) collective-permute-start(f32[1,3,128]{2,0,1:T(1,128)S(1)} %slice_bitcast_fusion.7), channel_id=1, source_target_pairs={{60,0},{0,4},{4,8},{8,12},{12,16},{16,20},{20,24},{24,28},{28,32},... | collective-permute-start | bytes 4616 | tf_op jit(solution)/shard_map/ppermute | solution.py:16
  170.1 5.5 collective-permute-start.10
  172.0 13.8 %collective-permute-start.15 = (f32[1,3,128]{2,0,1:T(1,128)S(1)}, f32[1,3,128]{2,0,1:T(1,128)S(1)}, u32[]{:S(2)}, u32[]{:S(2)}) collective-permute-start(f32[1,3,128]{2,0,1:T(1,128)S(1)} %slice_bitcast_fusion.6), channel_id=1, source_target_pairs={{4,0},{8,4},{12,8},{16,12},{20,16},{24,20},{28,24},{32,28},{36,32}... | collective-permute-start | bytes 4616 | tf_op jit(solution)/shard_map/ppermute | solution.py:16
  175.6 11.1 %collective-permute-start.11 = (f32[1,128,128]{2,1,0:T(8,128)S(1)}, f32[1,128,128]{2,1,0:T(8,128)S(1)}, u32[]{:S(2)}, u32[]{:S(2)}) collective-permute-start(f32[1,128,128]{2,1,0:T(8,128)S(1)} %slice_bitcast_fusion.2), channel_id=1, source_target_pairs={{4,0},{8,4},{12,8},{16,12},{20,16},{24,20},{28,24},{32,28},{36,32}... | collective-permute-start | bytes 196616 | tf_op jit(solution)/shard_map/ppermute | solution.py:16
  186.8 0.9 copy-start.4
  186.8 0.9 copy-start.6
  684.4 1.6 copy-start.7
Sparse Core Ops, SparseCore 0:
  188.6 318.1 all-reduce.5
where the time goes:
time: 699 us; the launch traced here: 694 us
  blocking collectives  496 us (71%)
  starting transfers between devices  106 us (15%)
  waiting for transfers between devices  36.2 us (5%)
  matrix products  22.2 us (3%)
  between operations  15.2 us (2%)
  local copies, waits for them, and re-layouts  10.5 us (2%)
  other arithmetic  7.97 us (1%)
    psum x1, blocking collectives, on_device(): lax.psum((grad_wvalue, grad_wradial, grad_gain, grad_wout), ('gx', 'gy'))  496 us
    ppermute x8, starting transfers between devices, passed_along(): return lax.ppermute(block, axis, route)  49.8 us
    ppermute x8, waiting for transfers between devices, passed_along(): return lax.ppermute(block, axis, route)  34.5 us
    ppermute x4, starting transfers between devices, with_halo(): lax.ppermute(lax.slice_in_dim(block, block.shape[dim] - width, None, axis...  31.9 us
    ppermute x4, starting transfers between devices, with_halo(): lax.ppermute(lax.slice_in_dim(block, 0, width, axis=dim), axis, backward)  24.1 us
  transfers between devices with their start and end apart: 17, of which 4 were waited for; matrix products, arithmetic and copies ran while one was open for 1% of the time, Pallas kernels for 0%

commit v1 on v0

v1 whole, which is shorter than its diff:
```python
import jax
import jax.numpy as jnp
from jax import lax
from jax.experimental import pallas as pl
from jax.experimental.pallas import tpu as pltpu
from jax.sharding import PartitionSpec as P

MESH = pl.DeviceIdType.MESH
F32 = jnp.float32
BF16 = jnp.bfloat16
HZ = 6.0
SOFTEN = 0.01
N = 128
K = 8
NX = 8
NY = 16
GAMMA = 24.5
FAR = 1000.0
POS, VAL, GRAD = 0, 1, 2
ROWS = 16

FIRST = (
    ((0, 1), (1, 1), "O"),
    ((0, 2), (1, 2), "O"),
    ((0, 1), (0, 3), "W"),
    ((0, 2), (0, 0), "E"),
)
RELAY = {
    1: (((1, 1), (2, 1), "P"), ((1, 1), (1, 3), "W"), ((1, 1), (2, 3), "PW")),
    2: (((1, 2), (2, 2), "P"), ((1, 2), (1, 0), "E"), ((1, 2), (2, 0), "PE")),
}


def dot(a, b, dims=((1,), (0,)), precision=None):
    return lax.dot_general(a, b, (dims, ((), ())), precision=precision, preferred_element_type=F32)


def kernel(
    feat, pos, types, counts, w_value, w_radial, type_gain, w_out, cot,
    out_feat, grad_feat, grad_pos, grad_wvalue, grad_wradial, grad_gain, grad_wout,
    hp, hc, hg, own, ebuf, usum, sbuf, lhs, pacc, proj, gain, onehot,
    ar_src, ar_one, ar_mid, ar_two, ar_three,
    send_sem, recv_sem, ar_send, ar_recv,
):
    gx = lax.axis_index("gx")
    gy = lax.axis_index("gy")
    zh = lax.rem(gx, 2)
    yy = gx // 2
    side = 1 - 2 * zh
    side_f = side.astype(F32)
    west, east = lax.rem(gy + NY - 1, NY), lax.rem(gy + 1, NY)
    across = lax.rem(gx + side + NX, NX)
    beyond = lax.rem(gx + 2 * side + NX, NX)
    behind = lax.rem(gx - 2 * side + NX, NX)
    dev = {
        "O": (across, gy), "W": (gx, west), "E": (gx, east), "P": (beyond, gy),
        "PW": (beyond, west), "PE": (beyond, east),
        "Q": (behind, gy), "QW": (behind, west), "QE": (behind, east),
    }
    dev = {name: {"gx": x, "gy": y} for name, (x, y) in dev.items()}
    quad = gy // 4
    q_me = yy * 4 + lax.rem(gy, 4)
    p_me = zh * 4 + quad

    def group_one(q):
        return {"gx": 2 * (q // 4) + zh, "gy": quad * 4 + lax.rem(q, 4)}

    def group_two(p):
        return {"gx": 2 * yy + p // 4, "gy": lax.rem(p, 4) * 4 + lax.rem(gy, 4)}

    barrier = pltpu.get_barrier_semaphore()
    for name in dev:
        pl.semaphore_signal(barrier, inc=1, device_id=dev[name], device_id_type=MESH)

    @pl.loop(1, 16)
    def _(d):
        pl.semaphore_signal(barrier, inc=1, device_id=group_one(lax.rem(q_me + d, 16)), device_id_type=MESH)

    @pl.loop(1, 8)
    def _(d):
        pl.semaphore_signal(barrier, inc=1, device_id=group_two(lax.rem(p_me + d, 8)), device_id_type=MESH)

    lane = lax.broadcasted_iota(jnp.int32, (1, N), 1)
    for c in range(2):
        missing = jnp.where(lane < counts[0, c], 0.0, FAR)
        x, y, z = (pos[0, c, n : n + 1, :] for n in range(3))
        z = z * HZ
        hp[0, :, (1 + c) * N : (2 + c) * N] = jnp.concatenate([x, y, z + missing, jnp.zeros((5, N), F32)], axis=0)
        for n, row in enumerate((x, y, z - missing)):
            own[c, n] = jnp.broadcast_to(row, (N, N)).T
    kind_of = lax.broadcasted_iota(jnp.int32, (16, N), 0)
    for c in range(2):
        hot = jnp.where(kind_of == types[0, c : c + 1, :], 1.0, 0.0)
        onehot[c] = hot
        gain[c] = dot(hot, type_gain[...], ((0,), (0,)), lax.Precision.HIGHEST)
        proj[c] = dot(feat[0, c], w_value[...])
        hc[0, (1 + c) * N : (2 + c) * N, :] = (proj[c] * gain[c]).astype(BF16)

    def slot(kind, place):
        role, column = place
        if kind == POS:
            return hp.at[role, :, column * N : (column + 1) * N]
        return (hc if kind == VAL else hg).at[role, column * N : (column + 1) * N, :]

    sent = []

    def send(kind, messages):
        for src, dst, to in messages:
            copy = pltpu.make_async_remote_copy(
                src_ref=slot(kind, src),
                dst_ref=slot(kind, dst),
                send_sem=send_sem.at[len(sent)],
                recv_sem=recv_sem.at[kind, dst[0] * 4 + dst[1]],
                device_id=dev[to],
                device_id_type=MESH,
            )
            copy.start()
            sent.append(copy)

    def arrive(kind, *places):
        for place in places:
            pltpu.make_async_remote_copy(
                src_ref=slot(kind, place),
                dst_ref=slot(kind, place),
                send_sem=send_sem.at[0],
                recv_sem=recv_sem.at[kind, place[0] * 4 + place[1]],
                device_id=dev["O"],
                device_id_type=MESH,
            ).wait_recv()

    pl.semaphore_wait(barrier, len(dev) + 15 + 7)
    send(POS, FIRST)
    send(VAL, FIRST)

    window = lax.broadcasted_iota(jnp.int32, (1, 3 * N), 1)
    shift_y = (window // N - 1).astype(F32)

    def near(c, role):
        block = hp[role, :, c * N : (c + 3) * N]
        shift_x = (0.0, side_f, -side_f)[role]
        return block[0:1] + shift_x, block[1:2] + shift_y, block[2:3]

    def geometry(c, role, near_rows, i0):
        deltas = []
        for n in range(3):
            mine = own[c, n, pl.ds(i0, ROWS), :]
            deltas.append(near_rows[n] - jnp.concatenate([mine] * 3, axis=1))
        dx, dy, dz = deltas
        dist = dx * dx + dy * dy + dz * dz
        if role == 0:
            row = lax.broadcasted_iota(jnp.int32, (ROWS, 3 * N), 0) + (i0 + N)
            col = lax.broadcasted_iota(jnp.int32, (ROWS, 3 * N), 1)
            dist = jnp.where(row == col, 2.0, dist)
        inside = jnp.maximum(1.0 - dist, 0.0)
        soft = (1.0 + SOFTEN) - inside
        inverse = lax.rsqrt(soft)
        ratio = jnp.exp((K - 1.0) * (soft * inverse))
        base = jnp.exp(-GAMMA * soft)
        return deltas, inside, inverse, ratio, base

    def weights(c, role):
        near_rows = near(c, role)

        @pl.loop(0, N // ROWS)
        def _(i):
            i0 = pl.multiple_of(i * ROWS, ROWS)
            _, inside, _, ratio, base = geometry(c, role, near_rows, i0)
            value = inside * inside * base
            for k in range(K):
                ebuf[c, role, k, pl.ds(i0, ROWS), :] = value.astype(BF16)
                if k < K - 1:
                    value = value * ratio

    def gather(c, role, table, first):
        got = dot(ebuf[c, role].reshape(K * N, 3 * N), table[role, c * N : (c + 3) * N, :]).reshape(K, N, N)
        if first:
            usum[c] = got
        else:
            usum[c] += got

    basis = lax.broadcasted_iota(jnp.int32, (K, N), 0).astype(F32)
    fold = jnp.exp(-0.5 * basis * basis)
    wk = w_radial[...] * fold

    arrive(POS, (0, 0), (0, 3))
    for c in range(2):
        weights(c, 0)
    for col in (1, 2):
        arrive(POS, (1, col))
        send(POS, RELAY[col])
    for c in range(2):
        value = hc[0, (1 + c) * N : (2 + c) * N, :].astype(F32)
        for k in range(K):
            lhs[c, k, :, N:] = (value * wk[k : k + 1]).astype(BF16)
    arrive(VAL, (0, 0), (0, 3))
    for c in range(2):
        gather(c, 0, hc, True)
    arrive(POS, (1, 0), (1, 3))
    for c in range(2):
        weights(c, 1)
    for col in (1, 2):
        arrive(VAL, (1, col))
        send(VAL, RELAY[col])
    arrive(POS, (2, 0), (2, 1), (2, 2), (2, 3))
    for c in range(2):
        weights(c, 2)
    arrive(VAL, (1, 0), (1, 3))
    for c in range(2):
        gather(c, 1, hc, False)
    arrive(VAL, (2, 0), (2, 1), (2, 2), (2, 3))
    for c in range(2):
        gather(c, 2, hc, False)

    pre = []
    halves = []
    for c in range(2):
        total = usum[c, 0] * wk[0:1]
        for k in range(1, K):
            total = total + usum[c, k] * wk[k : k + 1]
        halves.append(total.astype(BF16))
        pre.append(dot(halves[c], w_out[...]))
    grad_pre = []
    sigs = []
    for c in range(2):
        sig = jax.nn.sigmoid(pre[c])
        sigs.append(sig)
        grad_pre.append((cot[0, c].astype(F32) * sig * (1.0 + pre[c] * (1.0 - sig))).astype(BF16))
        hg[0, (1 + c) * N : (2 + c) * N, :] = dot(grad_pre[c], w_out[...], ((1,), (1,))).astype(BF16)
    send(GRAD, FIRST)
    for c in range(2):
        out_feat[0, c] = (feat[0, c].astype(F32) + pre[c] * sigs[c]).astype(BF16)
    wout_part = dot(halves[0], grad_pre[0], ((0,), (0,))) + dot(halves[1], grad_pre[1], ((0,), (0,)))
    grad_agg = [hg[0, (1 + c) * N : (2 + c) * N, :].astype(F32) for c in range(2)]
    rows = []
    for k in range(K):
        rows.append(jnp.sum(grad_agg[0] * usum[0, k] + grad_agg[1] * usum[1, k], axis=0, keepdims=True))
    wradial_part = jnp.concatenate(rows, axis=0) * fold

    def spread(a, main, small):
        for q in range(16):
            extra = jnp.broadcast_to(small[q % small.shape[0] : q % small.shape[0] + 1], (8, N))
            ar_src[a, q] = jnp.concatenate([main[8 * q : 8 * q + 8], extra], axis=0).astype(BF16)
        ar_one[a, pl.ds(q_me, 1)] = ar_src[a, pl.ds(q_me, 1)]

        @pl.loop(1, 16)
        def _(d):
            q = lax.rem(q_me + d, 16)
            pltpu.make_async_remote_copy(
                src_ref=ar_src.at[a, q], dst_ref=ar_one.at[a, q_me],
                send_sem=ar_send.at[a, 0], recv_sem=ar_recv.at[a, 0],
                device_id=group_one(q), device_id_type=MESH,
            ).start()

    def batch(buffer, a, count, phase):
        return pltpu.make_async_remote_copy(
            src_ref=buffer.at[a, pl.ds(0, count)], dst_ref=buffer.at[a, pl.ds(0, count)],
            send_sem=ar_send.at[a, phase], recv_sem=ar_recv.at[a, phase],
            device_id=dev["O"], device_id_type=MESH,
        )

    def middle(a):
        batch(ar_one, a, 15, 0).wait_recv()
        ar_mid[a] = jnp.sum(ar_one[a].astype(F32), axis=0).astype(BF16)
        ar_two[a, pl.ds(p_me, 1)] = ar_mid[a][None]

        @pl.loop(1, 8)
        def _(d):
            pltpu.make_async_remote_copy(
                src_ref=ar_mid.at[a], dst_ref=ar_two.at[a, p_me],
                send_sem=ar_send.at[a, 1], recv_sem=ar_recv.at[a, 1],
                device_id=group_two(lax.rem(p_me + d, 8)), device_id_type=MESH,
            ).start()

    def collect(a):
        batch(ar_two, a, 7, 1).wait_recv()
        final = jnp.sum(ar_two[a].astype(F32), axis=0).astype(BF16)
        ar_three[a, pl.ds(q_me, 1)] = final[None]

        @pl.loop(1, 16)
        def _(d):
            pltpu.make_async_remote_copy(
                src_ref=ar_three.at[a, q_me], dst_ref=ar_three.at[a, q_me],
                send_sem=ar_send.at[a, 2], recv_sem=ar_recv.at[a, 2],
                device_id=group_one(lax.rem(q_me + d, 16)), device_id_type=MESH,
            ).start()

    def finish(a, main, small):
        batch(ar_three, a, 15, 2).wait_recv()
        for q in range(16):
            chunk = ar_three[a, q].astype(F32)
            main[8 * q : 8 * q + 8, :] = chunk[0:8]
            if q < small.shape[0]:
                small[q : q + 1, :] = chunk[8:9]

    spread(0, wout_part, wradial_part)
    for c in range(2):
        for k in range(K):
            lhs[c, k, :, :N] = (grad_agg[c] * wk[k : k + 1]).astype(BF16)
        pacc[c] = jnp.zeros((3, N, N), F32)

    def pulls(c, role):
        both = jnp.concatenate([hc[role, c * N : (c + 3) * N, :], hg[role, c * N : (c + 3) * N, :]], axis=1)
        sbuf[...] = dot(lhs[c].reshape(K * N, 2 * N), both, ((1,), (1,))).reshape(K, N, 3 * N)
        near_rows = near(c, role)

        @pl.loop(0, N // ROWS)
        def _(i):
            i0 = pl.multiple_of(i * ROWS, ROWS)
            deltas, inside, inverse, ratio, base = geometry(c, role, near_rows, i0)
            total = sbuf[K - 1, pl.ds(i0, ROWS), :]
            slope = total
            for k in range(K - 2, -1, -1):
                total = total * ratio + sbuf[k, pl.ds(i0, ROWS), :]
                if k > 0:
                    slope = slope * ratio + total
            slope = slope * ratio
            pull = base * inside * (2.0 * total + GAMMA * inside * (total - slope * inverse * (1.0 / (K - 1.0))))
            for n in range(3):
                part = pull * deltas[n]
                pacc[c, n, pl.ds(i0, ROWS), :] += part[:, :N] + part[:, N : 2 * N] + part[:, 2 * N :]

    arrive(GRAD, (0, 0), (0, 3))
    for c in range(2):
        gather(c, 0, hg, True)
    for c in range(2):
        pulls(c, 0)
    middle(0)
    for col in (1, 2):
        arrive(GRAD, (1, col))
        send(GRAD, RELAY[col])
    collect(0)
    arrive(GRAD, (1, 0), (1, 3))
    for c in range(2):
        gather(c, 1, hg, False)
    for c in range(2):
        pulls(c, 1)
    arrive(GRAD, (2, 0), (2, 1), (2, 2), (2, 3))
    for c in range(2):
        gather(c, 2, hg, False)

    value_part = jnp.zeros((N, N), F32)
    gain_part = jnp.zeros((16, N), F32)
    back = []
    for c in range(2):
        total = usum[c, 0] * wk[0:1]
        for k in range(1, K):
            total = total + usum[c, k] * wk[k : k + 1]
        half = (total * gain[c]).astype(BF16)
        back.append(half)
        value_part = value_part + dot(feat[0, c], half, ((0,), (0,)))
        gain_part = gain_part + dot(onehot[c], total * proj[c], precision=lax.Precision.HIGHEST)
    spread(1, value_part, gain_part)
    pulls(0, 2)
    middle(1)
    pulls(1, 2)
    collect(1)
    for c in range(2):
        change = dot(back[c], w_value[...], ((1,), (1,)))
        grad_feat[0, c] = (cot[0, c].astype(F32) + change).astype(BF16)
        for n in range(3):
            scale = 2.0 * (HZ if n == 2 else 1.0)
            grad_pos[0, c, n : n + 1, :] = jnp.sum(pacc[c, n].T, axis=0, keepdims=True) * scale
    finish(0, grad_wout, grad_wradial)
    finish(1, grad_wvalue, grad_gain)
    for copy in sent:
        copy.wait_send()
    for a in range(2):
        batch(ar_one, a, 15, 0).wait_send()
        batch(ar_two, a, 7, 1).wait_send()
        batch(ar_three, a, 15, 2).wait_send()


def on_device(features, positions, bead_types, cell_counts, w_value, w_radial, type_gain, w_out, cotangent):
    vmem = pl.BlockSpec(memory_space=pltpu.VMEM)
    smem = pl.BlockSpec(memory_space=pltpu.SMEM)
    shape = jax.ShapeDtypeStruct
    return pl.pallas_call(
        kernel,
        out_shape=(
            shape((1, 2, N, N), BF16),
            shape((1, 2, N, N), BF16),
            shape((1, 2, 3, N), F32),
            shape((N, N), F32),
            shape((K, N), F32),
            shape((16, N), F32),
            shape((N, N), F32),
        ),
        in_specs=[vmem, vmem, vmem, smem, vmem, vmem, vmem, vmem, vmem],
        out_specs=(vmem,) * 7,
        scratch_shapes=[
            pltpu.VMEM((3, 8, 4 * N), F32),
            pltpu.VMEM((3, 4 * N, N), BF16),
            pltpu.VMEM((3, 4 * N, N), BF16),
            pltpu.VMEM((2, 3, N, N), F32),
            pltpu.VMEM((2, 3, K, N, 3 * N), BF16),
            pltpu.VMEM((2, K, N, N), F32),
            pltpu.VMEM((K, N, 3 * N), F32),
            pltpu.VMEM((2, K, N, 2 * N), BF16),
            pltpu.VMEM((2, 3, N, N), F32),
            pltpu.VMEM((2, N, N), F32),
            pltpu.VMEM((2, N, N), F32),
            pltpu.VMEM((2, 16, N), F32),
            pltpu.VMEM((2, 16, 16, N), BF16),
            pltpu.VMEM((2, 16, 16, N), BF16),
            pltpu.VMEM((2, 16, N), BF16),
            pltpu.VMEM((2, 8, 16, N), BF16),
            pltpu.VMEM((2, 16, 16, N), BF16),
            pltpu.SemaphoreType.DMA((30,)),
            pltpu.SemaphoreType.DMA((3, 12)),
            pltpu.SemaphoreType.DMA((2, 3)),
            pltpu.SemaphoreType.DMA((2, 3)),
        ],
        compiler_params=pltpu.CompilerParams(
            collective_id=0, has_side_effects=True, vmem_limit_bytes=40 * 1024 * 1024
        ),
        cost_estimate=pl.CostEstimate(flops=3_000_000_000, bytes_accessed=1_000_000, transcendentals=4_000_000),
    )(features, positions, bead_types, cell_counts, w_value, w_radial, type_gain, w_out, cotangent)


def solution(mesh):
    cells = P(("frame", "gx"), "gy", None, None)
    return jax.shard_map(
        on_device,
        mesh=mesh,
        in_specs=(cells, cells, P(("frame", "gx"), "gy", None), P(("frame", "gx"), "gy"), P(), P(), P(), P(), cells),
        out_specs=(cells, cells, cells) + (P("frame", None),) * 4,
        check_vma=False,
    )
```

time: 699 us -> 87.1 us (0.12)
  blocking collectives: 496 us -> 0 us
  starting transfers between devices: 106 us -> 0 us
  Pallas kernels: 0 us -> 77.1 us
  waiting for transfers between devices: 36.2 us -> 0 us
  matrix products: 22.2 us -> 0 us
  between operations: 15.2 us -> 0.69 us
  other arithmetic: 7.97 us -> 0 us
    psum x1 -> x0, blocking collectives: 496 us -> none  [on_device(): lax.psum((grad_wvalue, grad_wradial, grad_gain, grad_wout), ('gx', 'gy'))]
    ppermute x16 -> x0, starting transfers between devices: 106 us -> none  [the longest x8 49.8 us: passed_along(): return lax.ppermute(block, axis, route)]
    pallas_call x0 -> x1, Pallas kernels: none -> 77.1 us  [on_device(): pl.pallas_call(kernel, out_shape=(shape((1, 2, N, N), BF16), shape((1, 2,...]
    ppermute x16 -> x0, waiting for transfers between devices: 36.2 us -> none  [the longest x8 34.5 us: passed_along(): return lax.ppermute(block, axis, route)]
    dot_general x35 -> x0, matrix products: 22.2 us -> none  [the longest x9 8.02 us: on_device(): jnp.einsum('abkij,abkic->abjc', weights, scaled, preferred_element_type=j...]
  transfers between devices with their start and end apart: 17 -> 0, of which waited for: 4 -> 0; matrix products, arithmetic and copies ran while one was open for 1% -> 0% of each run, Pallas kernels for 0% -> 0%
where the time goes in v1:
time: 87.1 us; the launch traced here: 86.6 us
  Pallas kernels  77.1 us (89%)
  local copies, waits for them, and re-layouts  8.89 us (10%)
    pallas_call x1, Pallas kernels, on_device(): pl.pallas_call(kernel, out_shape=(shape((1, 2, N, N), BF16), shape((1, 2,...  77.1 us
    unnamed x23, local copies, waits for them, and re-layouts  8.31 us

profile of v1, /device:TPU:1, one launch (start us, length us, event | category | flops | bytes accessed | tf_op | source)
XLA Modules:
  0.0 86.6 jit_solution(3784637082660493455)
XLA Ops:
  0.6 0.0 copy-start.5
  0.6 0.0 copy-start.7
  0.7 0.0 copy-start.6
  0.7 0.7 copy.16.pos
  1.4 0.0 copy-done.5
  1.4 0.0 copy-done.7
  1.4 0.0 copy-done.6
  1.4 0.0 copy-start
  1.4 0.8 copy-done
  2.2 0.0 copy-start.1
  2.2 0.8 copy-done.1
  3.1 0.0 copy-start.2
  3.1 0.8 copy-done.2
  3.8 0.0 copy-start.3
  3.8 0.8 copy-done.3
  4.6 0.0 copy-start.4
  4.6 0.7 copy-done.4
  5.3 77.1 %shard_map.144 = (bf16[1,2,128,128]{3,2,1,0:T(8,128)(2,1)S(1)}, bf16[1,2,128,128]{3,2,1,0:T(8,128)(2,1)S(1)}, f32[1,2,3,128]{3,2,1,0:T(4,128)S(1)}, f32[128,128]...) custom-call(bf16[1,2,128,128]{3,2,1,0:T(8,128)(2,1)S(1)} %copy-done, ...), custom_call_target="tpu_custom_call" | custom-call | flops 3000000000 | bytes 1000000 | tf_op jit(solution)/shard_map/pallas_call | solution.py:377
  82.3 0.6 copy.17
  82.9 0.6 copy.24
  83.6 0.6 copy.25
  84.2 0.6 copy.26
  84.8 0.6 copy.27
  85.4 0.6 copy.28
  86.0 0.6 copy.29
Async XLA Ops:
  0.6 0.7 copy-start.5
  0.6 0.7 copy-start.7
  0.7 0.7 copy-start.6
  1.4 0.8 copy-start
  2.2 0.8 copy-start.1
  3.1 0.8 copy-start.2
  3.8 0.8 copy-start.3
  4.6 0.7 copy-start.4

commit v2 on v1

v2 whole, which is shorter than its diff:
```python
import jax
import jax.numpy as jnp
from jax import lax
from jax.experimental import pallas as pl
from jax.experimental.pallas import tpu as pltpu
from jax.sharding import PartitionSpec as P

MESH = pl.DeviceIdType.MESH
F32 = jnp.float32
BF16 = jnp.bfloat16
EXACT = lax.Precision.HIGHEST
HZ = 6.0
SOFTEN = 0.01
N = 128
K = 8
NX = 8
NY = 16
GAMMA = 24.5
FAR = 1000.0
POS, VAL, GRAD = 0, 1, 2
ROWS = 16
COMM = True

FIRST = (
    ((0, 1), (1, 1), "O", "all"),
    ((0, 2), (1, 2), "O", "all"),
    ((0, 1), (0, 3), "W", "all"),
    ((0, 2), (0, 0), "E", "all"),
    ((0, 1), (1, 3), "OW", "first"),
    ((0, 1), (2, 3), "RW", "first"),
    ((0, 2), (1, 0), "OE", "last"),
    ((0, 2), (2, 0), "RE", "last"),
)
RELAY = {
    1: (((1, 1), (2, 1), "P", "all"), ((1, 1), (1, 3), "W", "not first"), ((1, 1), (2, 3), "PW", "not first")),
    2: (((1, 2), (2, 2), "P", "all"), ((1, 2), (1, 0), "E", "not last"), ((1, 2), (2, 0), "PE", "not last")),
}


def dot(a, b, dims=((1,), (0,)), precision=None):
    return lax.dot_general(a, b, (dims, ((), ())), precision=precision, preferred_element_type=F32)


def kernel(
    feat_in, pos_in, types_in, counts_in, w_value_in, w_radial_in, type_gain_in, w_out_in, cot_in,
    out_feat, grad_feat, grad_pos, grad_wvalue, grad_wradial, grad_gain, grad_wout,
    hp, hf, hc, hg, own, ebuf, geo, usum, sbuf, lhs, pacc, proj, gain, onehot, wkt, sct, vt,
    pos, types, counts, w_value, w_radial, type_gain, w_out, cot,
    ar_src, ar_one, ar_mid, ar_two, ar_three,
    load_sem, send_sem, recv_sem, ar_send, ar_recv,
):
    gx = lax.axis_index("gx")
    gy = lax.axis_index("gy")
    zh = lax.rem(gx, 2)
    yy = gx // 2
    side = 1 - 2 * zh
    side_f = side.astype(F32)
    west, east = lax.rem(gy + NY - 1, NY), lax.rem(gy + 1, NY)
    across = lax.rem(gx + side + NX, NX)
    other = lax.rem(gx - side + NX, NX)
    beyond = lax.rem(gx + 2 * side + NX, NX)
    behind = lax.rem(gx - 2 * side + NX, NX)
    dev = {
        "O": (across, gy), "OW": (across, west), "OE": (across, east),
        "RW": (other, west), "RE": (other, east),
        "W": (gx, west), "E": (gx, east),
        "P": (beyond, gy), "PW": (beyond, west), "PE": (beyond, east),
        "Q": (behind, gy), "QW": (behind, west), "QE": (behind, east),
    }
    dev = {name: {"gx": x, "gy": y} for name, (x, y) in dev.items()}
    quad = gy // 4
    q_me = yy * 4 + lax.rem(gy, 4)
    p_me = zh * 4 + quad

    def group_one(q):
        return {"gx": 2 * (q // 4) + zh, "gy": quad * 4 + lax.rem(q, 4)}

    def group_two(p):
        return {"gx": 2 * yy + p // 4, "gy": lax.rem(p, 4) * 4 + lax.rem(gy, 4)}

    barrier = pltpu.get_barrier_semaphore()
    if COMM:
        for name in dev:
            pl.semaphore_signal(barrier, inc=1, device_id=dev[name], device_id_type=MESH)

        @pl.loop(1, 16)
        def _(d):
            pl.semaphore_signal(barrier, inc=1, device_id=group_one(lax.rem(q_me + d, 16)), device_id_type=MESH)

        @pl.loop(1, 8)
        def _(d):
            pl.semaphore_signal(barrier, inc=1, device_id=group_two(lax.rem(p_me + d, 8)), device_id_type=MESH)

    loads = []
    for n, (src, dst) in enumerate((
        (pos_in, pos), (types_in, types), (counts_in, counts), (w_radial_in, w_radial),
        (feat_in.at[0, 0], hf.at[0, N : 2 * N, :]), (feat_in.at[0, 1], hf.at[0, 2 * N : 3 * N, :]),
        (type_gain_in, type_gain), (w_value_in, w_value), (w_out_in, w_out), (cot_in, cot),
    )):
        loads.append(pltpu.make_async_copy(src, dst, load_sem.at[n]))
        loads[-1].start()

    for load in loads[:4]:
        load.wait()
    lane = lax.broadcasted_iota(jnp.int32, (1, N), 1)
    for c in range(2):
        missing = jnp.where(lane < counts[:, c : c + 1], 0.0, FAR)
        x, y, z = (pos[0, n, c : c + 1, :] for n in range(3))
        z = z * HZ
        kind = types[0, c : c + 1, :].astype(F32)
        hp[0, :, (1 + c) * N : (2 + c) * N] = jnp.concatenate(
            [x, y, z + missing, kind, jnp.zeros((4, N), F32)], axis=0
        )
        for n, row in enumerate((x, y, z - missing)):
            own[c, n] = jnp.broadcast_to(row, (N, N)).T
    basis = lax.broadcasted_iota(jnp.int32, (K, N), 0).astype(F32)
    fold = jnp.exp(-0.5 * basis * basis)
    wk = w_radial[...] * fold
    for k in range(K):
        wkt[k] = jnp.broadcast_to(wk[k : k + 1], (N, N)).T
    for load in loads[4:]:
        load.wait()

    def slot(kind, place):
        role, column = place
        if kind == POS:
            return hp.at[role, :, column * N : (column + 1) * N]
        return (hf if kind == VAL else hg).at[role, column * N : (column + 1) * N, :]

    sent = []

    def where_sent(who, act):
        if who == "all":
            act()
        else:
            pl.when({
                "first": gy == 0, "not first": gy != 0, "last": gy == NY - 1, "not last": gy != NY - 1
            }[who])(act)

    def send(kind, messages):
        if not COMM:
            return
        for src, dst, to, who in messages:
            copy = pltpu.make_async_remote_copy(
                src_ref=slot(kind, src),
                dst_ref=slot(kind, dst),
                send_sem=send_sem.at[len(sent)],
                recv_sem=recv_sem.at[kind, dst[0] * 4 + dst[1]],
                device_id=dev[to],
                device_id_type=MESH,
            )
            where_sent(who, copy.start)
            sent.append((who, copy))

    def arrive(kind, *places):
        if not COMM:
            return
        for place in places:
            pltpu.make_async_remote_copy(
                src_ref=slot(kind, place),
                dst_ref=slot(kind, place),
                send_sem=send_sem.at[0],
                recv_sem=recv_sem.at[kind, place[0] * 4 + place[1]],
                device_id=dev["O"],
                device_id_type=MESH,
            ).wait_recv()

    if COMM:
        pl.semaphore_wait(barrier, len(dev) + 15 + 7)
    send(POS, FIRST)
    send(VAL, FIRST)

    window = lax.broadcasted_iota(jnp.int32, (1, 3 * N), 1)
    shift_y = (window // N - 1).astype(F32)

    def near(c, role):
        block = hp[role, :, c * N : (c + 3) * N]
        shift_x = (0.0, side_f, -side_f)[role]
        return block[0:1] + shift_x, block[1:2] + shift_y, block[2:3]

    def deltas_of(c, near_rows, i0):
        deltas = []
        for n in range(3):
            mine = own[c, n, pl.ds(i0, ROWS), :]
            deltas.append(near_rows[n] - jnp.concatenate([mine] * 3, axis=1))
        return deltas

    def weights(c, role):
        near_rows = near(c, role)

        @pl.loop(0, N // ROWS)
        def _(i):
            i0 = pl.multiple_of(i * ROWS, ROWS)
            dx, dy, dz = deltas_of(c, near_rows, i0)
            dist = dx * dx + dy * dy + dz * dz
            if role == 0:
                row = lax.broadcasted_iota(jnp.int32, (ROWS, 3 * N), 0) + (i0 + N)
                col = lax.broadcasted_iota(jnp.int32, (ROWS, 3 * N), 1)
                dist = jnp.where(row == col, 2.0, dist)
            inside = jnp.maximum(1.0 - dist, 0.0)
            soft = (1.0 + SOFTEN) - inside
            inverse = lax.rsqrt(soft)
            ratio = jnp.exp((K - 1.0) * (soft * inverse))
            lead = inside * jnp.exp(-GAMMA * soft)
            value = inside * lead
            geo[c, role, 0, pl.ds(i0, ROWS), :] = ratio
            geo[c, role, 1, pl.ds(i0, ROWS), :] = 2.0 * lead + GAMMA * value
            geo[c, role, 2, pl.ds(i0, ROWS), :] = value * inverse * (GAMMA / (K - 1.0))
            for k in range(K):
                ebuf[c, role, k, pl.ds(i0, ROWS), :] = value.astype(BF16)
                if k < K - 1:
                    value = value * ratio

    def gather(c, role, table, first):
        got = dot(ebuf[c, role].reshape(K * N, 3 * N), table[role, c * N : (c + 3) * N, :]).reshape(K, N, N)
        if first:
            usum[c] = got
        else:
            usum[c] += got

    kind_of = lax.broadcasted_iota(jnp.int32, (16, 4 * N), 0).astype(F32)

    def gains(role):
        hot = jnp.where(kind_of == hp[role, 3:4, :], 1.0, 0.0)
        onehot[role] = hot
        gain[role] = dot(hot, type_gain[...], ((0,), (0,)), EXACT)

    def values(role):
        projected = dot(hf[role], w_value[...])
        proj[role] = projected
        hc[role] = (projected * gain[role]).astype(BF16)

    arrive(POS, (0, 0), (0, 3))
    for c in range(2):
        weights(c, 0)
    gains(0)
    for col in (1, 2):
        arrive(POS, (1, col))
        send(POS, RELAY[col])
    arrive(VAL, (0, 0), (0, 3))
    values(0)
    for c in range(2):
        gather(c, 0, hc, True)
    for col in (1, 2):
        arrive(VAL, (1, col))
        send(VAL, RELAY[col])
    for c in range(2):
        value = hc[0, (1 + c) * N : (2 + c) * N, :].astype(F32)
        for k in range(K):
            lhs[c, k, :, N:] = (value * wk[k : k + 1]).astype(BF16)
    arrive(POS, (1, 0), (1, 3))
    for c in range(2):
        weights(c, 1)
    gains(1)
    arrive(POS, (2, 0), (2, 1), (2, 2), (2, 3))
    for c in range(2):
        weights(c, 2)
    gains(2)
    arrive(VAL, (1, 0), (1, 3))
    values(1)
    for c in range(2):
        gather(c, 1, hc, False)
    arrive(VAL, (2, 0), (2, 1), (2, 2), (2, 3))
    values(2)
    for c in range(2):
        gather(c, 2, hc, False)

    def own_rows(c):
        return slice((1 + c) * N, (2 + c) * N)

    pre = []
    halves = []
    for c in range(2):
        total = usum[c, 0] * wk[0:1]
        for k in range(1, K):
            total = total + usum[c, k] * wk[k : k + 1]
        halves.append(total.astype(BF16))
        pre.append(dot(halves[c], w_out[...]))
    grad_pre = []
    sigs = []
    grad_agg = []
    for c in range(2):
        sig = jax.nn.sigmoid(pre[c])
        sigs.append(sig)
        grad_pre.append((cot[0, c].astype(F32) * sig * (1.0 + pre[c] * (1.0 - sig))).astype(BF16))
        half = dot(grad_pre[c], w_out[...], ((1,), (1,))).astype(BF16)
        hg[0, own_rows(c), :] = half
        grad_agg.append(half.astype(F32))
    send(GRAD, FIRST)

    for c in range(2):
        flipped = grad_agg[c].T
        for k in range(K):
            sct[c, :, k * N : (k + 1) * N] = (flipped * wkt[k]).astype(BF16)
    for role in range(3):
        vt[role, :, 3 * N :] = jnp.zeros((N, N), F32)
        vt[role, :, : 3 * N] = dot(sct[0], ebuf[0, role].reshape(K * N, 3 * N))
        vt[role, :, N:] += dot(sct[1], ebuf[1, role].reshape(K * N, 3 * N))
    value_part = jnp.zeros((N, N), F32)
    gain_part = jnp.zeros((16, N), F32)
    for role in range(3):
        given = vt[role].T
        half = (given * gain[role]).astype(BF16)
        value_part = value_part + dot(hf[role], half, ((0,), (0,)))
        gain_part = gain_part + dot(onehot[role], given * proj[role], precision=EXACT)
    wout_part = dot(halves[0], grad_pre[0], ((0,), (0,))) + dot(halves[1], grad_pre[1], ((0,), (0,)))
    rows = []
    for k in range(K):
        rows.append(jnp.sum(grad_agg[0] * usum[0, k] + grad_agg[1] * usum[1, k], axis=0, keepdims=True))
    wradial_part = jnp.concatenate(rows, axis=0) * fold

    for q in range(16):
        own_q = slice(8 * q, 8 * q + 8)
        ar_src[q] = jnp.concatenate(
            [
                value_part[own_q],
                wout_part[own_q],
                jnp.broadcast_to(gain_part[q : q + 1], (8, N)),
                jnp.broadcast_to(wradial_part[q % K : q % K + 1], (8, N)),
            ],
            axis=0,
        ).astype(BF16)
    ar_one[pl.ds(q_me, 1)] = ar_src[pl.ds(q_me, 1)]

    def batch(buffer, count, phase):
        return pltpu.make_async_remote_copy(
            src_ref=buffer.at[pl.ds(0, count)], dst_ref=buffer.at[pl.ds(0, count)],
            send_sem=ar_send.at[phase], recv_sem=ar_recv.at[phase],
            device_id=dev["O"], device_id_type=MESH,
        )

    if COMM:
        @pl.loop(1, 16)
        def _(d):
            q = lax.rem(q_me + d, 16)
            pltpu.make_async_remote_copy(
                src_ref=ar_src.at[q], dst_ref=ar_one.at[q_me],
                send_sem=ar_send.at[0], recv_sem=ar_recv.at[0],
                device_id=group_one(q), device_id_type=MESH,
            ).start()

    def middle():
        if COMM:
            batch(ar_one, 15, 0).wait_recv()
        ar_mid[...] = jnp.sum(ar_one[...].astype(F32), axis=0).astype(BF16)
        ar_two[pl.ds(p_me, 1)] = ar_mid[...][None]
        if COMM:
            @pl.loop(1, 8)
            def _(d):
                pltpu.make_async_remote_copy(
                    src_ref=ar_mid, dst_ref=ar_two.at[p_me],
                    send_sem=ar_send.at[1], recv_sem=ar_recv.at[1],
                    device_id=group_two(lax.rem(p_me + d, 8)), device_id_type=MESH,
                ).start()

    def collect():
        if COMM:
            batch(ar_two, 7, 1).wait_recv()
        final = jnp.sum(ar_two[...].astype(F32), axis=0).astype(BF16)
        ar_three[pl.ds(q_me, 1)] = final[None]
        if COMM:
            @pl.loop(1, 16)
            def _(d):
                pltpu.make_async_remote_copy(
                    src_ref=ar_three.at[q_me], dst_ref=ar_three.at[q_me],
                    send_sem=ar_send.at[2], recv_sem=ar_recv.at[2],
                    device_id=group_one(lax.rem(q_me + d, 16)), device_id_type=MESH,
                ).start()

    def finish():
        if COMM:
            batch(ar_three, 15, 2).wait_recv()
        for q in range(16):
            chunk = ar_three[q].astype(F32)
            grad_wvalue[8 * q : 8 * q + 8, :] = chunk[0:8]
            grad_wout[8 * q : 8 * q + 8, :] = chunk[8:16]
            grad_gain[q : q + 1, :] = chunk[16:17]
            if q < K:
                grad_wradial[q : q + 1, :] = chunk[24:25]

    for c in range(2):
        for k in range(K):
            lhs[c, k, :, :N] = (grad_agg[c] * wk[k : k + 1]).astype(BF16)
        pacc[c] = jnp.zeros((3, N, N), F32)

    def pulls(c, role):
        span = slice(c * N, (c + 3) * N)
        both = jnp.concatenate([hc[role, span, :], hg[role, span, :]], axis=1)
        sbuf[...] = dot(lhs[c].reshape(K * N, 2 * N), both, ((1,), (1,))).reshape(K, N, 3 * N)
        near_rows = near(c, role)

        @pl.loop(0, N // ROWS)
        def _(i):
            i0 = pl.multiple_of(i * ROWS, ROWS)
            deltas = deltas_of(c, near_rows, i0)
            ratio = geo[c, role, 0, pl.ds(i0, ROWS), :]
            total = sbuf[K - 1, pl.ds(i0, ROWS), :]
            slope = total
            for k in range(K - 2, -1, -1):
                total = total * ratio + sbuf[k, pl.ds(i0, ROWS), :]
                if k > 0:
                    slope = slope * ratio + total
            slope = slope * ratio
            pull = geo[c, role, 1, pl.ds(i0, ROWS), :] * total - geo[c, role, 2, pl.ds(i0, ROWS), :] * slope
            for n in range(3):
                part = pull * deltas[n]
                pacc[c, n, pl.ds(i0, ROWS), :] += part[:, :N] + part[:, N : 2 * N] + part[:, 2 * N :]

    for c in range(2):
        out_feat[0, c] = (hf[0, own_rows(c), :].astype(F32) + pre[c] * sigs[c]).astype(BF16)
    arrive(GRAD, (0, 0), (0, 3))
    for c in range(2):
        gather(c, 0, hg, True)
    middle()
    for col in (1, 2):
        arrive(GRAD, (1, col))
        send(GRAD, RELAY[col])
    for c in range(2):
        pulls(c, 0)
    collect()
    arrive(GRAD, (1, 0), (1, 3))
    for c in range(2):
        gather(c, 1, hg, False)
    for c in range(2):
        pulls(c, 1)
    arrive(GRAD, (2, 0), (2, 1), (2, 2), (2, 3))
    for c in range(2):
        gather(c, 2, hg, False)
    for c in range(2):
        pulls(c, 2)

    for c in range(2):
        total = usum[c, 0] * wk[0:1]
        for k in range(1, K):
            total = total + usum[c, k] * wk[k : k + 1]
        back = (total * gain[0, own_rows(c), :]).astype(BF16)
        change = dot(back, w_value[...], ((1,), (1,)))
        grad_feat[0, c] = (cot[0, c].astype(F32) + change).astype(BF16)
        for n in range(3):
            scale = 2.0 * (HZ if n == 2 else 1.0)
            grad_pos[0, n, c : c + 1, :] = jnp.sum(pacc[c, n].T, axis=0, keepdims=True) * scale
    finish()
    if COMM:
        for who, copy in sent:
            where_sent(who, copy.wait_send)
        batch(ar_one, 15, 0).wait_send()
        batch(ar_two, 7, 1).wait_send()
        batch(ar_three, 15, 2).wait_send()


def store(*refs):
    count = len(refs) // 2
    sems = refs[-1]
    copies = [pltpu.make_async_copy(refs[n], refs[count + n], sems.at[n]) for n in range(count)]
    for copy in copies:
        copy.start()
    for copy in copies:
        copy.wait()


def on_device(features, positions, bead_types, cell_counts, w_value, w_radial, type_gain, w_out, cotangent):
    vmem = pl.BlockSpec(memory_space=pltpu.VMEM)
    anywhere = pl.BlockSpec(memory_space=pl.ANY)
    shape = jax.ShapeDtypeStruct
    shapes = (
        shape((1, 2, N, N), BF16),
        shape((1, 2, N, N), BF16),
        shape((1, 3, 2, N), F32),
        shape((N, N), F32),
        shape((K, N), F32),
        shape((16, N), F32),
        shape((N, N), F32),
    )
    results = pl.pallas_call(
        kernel,
        out_shape=shapes,
        in_specs=[pl.BlockSpec(memory_space=pltpu.HBM)] * 9,
        out_specs=(vmem,) * 7,
        scratch_shapes=[
            pltpu.VMEM((3, 8, 4 * N), F32),
            pltpu.VMEM((3, 4 * N, N), BF16),
            pltpu.VMEM((3, 4 * N, N), BF16),
            pltpu.VMEM((3, 4 * N, N), BF16),
            pltpu.VMEM((2, 3, N, N), F32),
            pltpu.VMEM((2, 3, K, N, 3 * N), BF16),
            pltpu.VMEM((2, 3, 3, N, 3 * N), F32),
            pltpu.VMEM((2, K, N, N), F32),
            pltpu.VMEM((K, N, 3 * N), F32),
            pltpu.VMEM((2, K, N, 2 * N), BF16),
            pltpu.VMEM((2, 3, N, N), F32),
            pltpu.VMEM((3, 4 * N, N), F32),
            pltpu.VMEM((3, 4 * N, N), F32),
            pltpu.VMEM((3, 16, 4 * N), F32),
            pltpu.VMEM((K, N, N), F32),
            pltpu.VMEM((2, N, K * N), BF16),
            pltpu.VMEM((3, N, 4 * N), F32),
            pltpu.VMEM((1, 3, 2, N), F32),
            pltpu.VMEM((1, 2, N), jnp.int32),
            pltpu.VMEM((1, 2), jnp.int32),
            pltpu.VMEM((N, N), BF16),
            pltpu.VMEM((K, N), F32),
            pltpu.VMEM((16, N), F32),
            pltpu.VMEM((N, N), BF16),
            pltpu.VMEM((1, 2, N, N), BF16),
            pltpu.VMEM((16, 32, N), BF16),
            pltpu.VMEM((16, 32, N), BF16),
            pltpu.VMEM((32, N), BF16),
            pltpu.VMEM((8, 32, N), BF16),
            pltpu.VMEM((16, 32, N), BF16),
            pltpu.SemaphoreType.DMA((10,)),
            pltpu.SemaphoreType.DMA((42,)),
            pltpu.SemaphoreType.DMA((3, 12)),
            pltpu.SemaphoreType.DMA((3,)),
            pltpu.SemaphoreType.DMA((3,)),
        ],
        compiler_params=pltpu.CompilerParams(
            collective_id=0, has_side_effects=True, vmem_limit_bytes=60 * 1024 * 1024
        ),
        cost_estimate=pl.CostEstimate(flops=4_000_000_000, bytes_accessed=1_000_000, transcendentals=4_000_000),
    )(features, positions.transpose(0, 2, 1, 3), bead_types, cell_counts, w_value, w_radial, type_gain, w_out, cotangent)
    out = pl.pallas_call(
        store,
        out_shape=shapes,
        in_specs=[anywhere] * 7,
        out_specs=(pl.BlockSpec(memory_space=pltpu.HBM),) * 7,
        scratch_shapes=[pltpu.SemaphoreType.DMA((7,))],
        compiler_params=pltpu.CompilerParams(vmem_limit_bytes=60 * 1024 * 1024),
    )(*results)
    return (out[0], out[1], out[2].transpose(0, 2, 1, 3)) + tuple(out[3:])


def solution(mesh):
    cells = P(("frame", "gx"), "gy", None, None)
    return jax.shard_map(
        on_device,
        mesh=mesh,
        in_specs=(cells, cells, P(("frame", "gx"), "gy", None), P(("frame", "gx"), "gy"), P(), P(), P(), P(), cells),
        out_specs=(cells, cells, cells) + (P("frame", None),) * 4,
        check_vma=False,
    )
```

time: 87.1 us -> 67.9 us (0.78)
  Pallas kernels: 77.1 us -> 67.1 us
  local copies, waits for them, and re-layouts: 8.89 us -> 0 us
    pallas_call x1 -> x2, Pallas kernels: 77.1 us -> 67.1 us  [the longest x1 57.5 us: on_device(): pl.pallas_call(kernel, out_shape=shapes, in_specs=[pl.BlockSpec(memory_sp...]
    unnamed x23 -> x0, local copies, waits for them, and re-layouts: 8.31 us -> none
where the time goes in v2:
time: 67.9 us; the launch traced here: 67.8 us
  Pallas kernels  67.1 us (99%)
    pallas_call x1, Pallas kernels, on_device(): pl.pallas_call(kernel, out_shape=shapes, in_specs=[pl.BlockSpec(memory_sp...  57.5 us
    pallas_call x1, Pallas kernels, on_device(): pl.pallas_call(store, out_shape=shapes, in_specs=[anywhere] * 7, out_spec...  9.57 us

profile of v2, /device:TPU:1, one launch (start us, length us, event | category | flops | bytes accessed | tf_op | source)
XLA Modules:
  0.0 67.8 jit_solution(13260523992864652529)
XLA Ops:
  0.6 57.5 %shard_map.144 = (bf16[1,2,128,128]{3,2,1,0:T(8,128)(2,1)}, bf16[1,2,128,128]{3,2,1,0:T(8,128)(2,1)}, f32[1,3,2,128]{3,2,1,0:T(2,128)}, f32[128,128]{1,0:T(8,128...) custom-call(bf16[1,2,128,128]{3,2,1,0:T(8,128)(2,1)} %feat_in.1, f32[1,3,2,128]{3,2,1,0:T(2,128)} %bitcast.2, ...), custom_call_target="tpu_custom_call" | custom-call | flops 4000000000 | bytes 1000000 | tf_op jit(solution)/shard_map/pallas_call | solution.py:474
  58.2 9.6 %shard_map.145 = (bf16[1,2,128,128]{3,2,1,0:T(8,128)(2,1)}, bf16[1,2,128,128]{3,2,1,0:T(8,128)(2,1)}, f32[1,3,2,128]{3,2,1,0:T(2,128)}, f32[128,128]{1,0:T(8,128...) custom-call(bf16[1,2,128,128]{3,2,1,0:T(8,128)(2,1)} %get-tuple-element.21.refs_0_, ...), custom_call_target="tpu_custom_call" | custom-call | tf_op jit(solution)/shard_map/pallas_call | solution.py:521

commit v3 on v2

--- a/solution.py
+++ b/solution.py
@@ -78,51 +78,45 @@
     def group_two(p):
         return {"gx": 2 * yy + p // 4, "gy": lax.rem(p, 4) * 4 + lax.rem(gy, 4)}
 
+    loads = [
+        pltpu.make_async_copy(src, dst, load_sem.at[n])
+        for n, (src, dst) in enumerate((
+            (pos_in, pos), (types_in, types), (counts_in, counts), (w_radial_in, w_radial),
+            (feat_in.at[0, 0], hf.at[0, N : 2 * N, :]), (feat_in.at[0, 1], hf.at[0, 2 * N : 3 * N, :]),
+            (type_gain_in, type_gain), (w_value_in, w_value), (w_out_in, w_out), (cot_in, cot),
+        ))
+    ]
+    for load in loads[:3]:
+        load.start()
     barrier = pltpu.get_barrier_semaphore()
     if COMM:
         for name in dev:
             pl.semaphore_signal(barrier, inc=1, device_id=dev[name], device_id_type=MESH)
-
-        @pl.loop(1, 16)
-        def _(d):
+        for d in range(1, 16):
             pl.semaphore_signal(barrier, inc=1, device_id=group_one(lax.rem(q_me + d, 16)), device_id_type=MESH)
-
-        @pl.loop(1, 8)
-        def _(d):
+        for d in range(1, 8):
             pl.semaphore_signal(barrier, inc=1, device_id=group_two(lax.rem(p_me + d, 8)), device_id_type=MESH)
-
-    loads = []
-    for n, (src, dst) in enumerate((
-        (pos_in, pos), (types_in, types), (counts_in, counts), (w_radial_in, w_radial),
-        (feat_in.at[0, 0], hf.at[0, N : 2 * N, :]), (feat_in.at[0, 1], hf.at[0, 2 * N : 3 * N, :]),
-        (type_gain_in, type_gain), (w_value_in, w_value), (w_out_in, w_out), (cot_in, cot),
-    )):
-        loads.append(pltpu.make_async_copy(src, dst, load_sem.at[n]))
-        loads[-1].start()
-
-    for load in loads[:4]:
+    for load in loads[3:]:
+        load.start()
+
+    for load in loads[:3]:
         load.wait()
     lane = lax.broadcasted_iota(jnp.int32, (1, N), 1)
+    near_z = []
     for c in range(2):
         missing = jnp.where(lane < counts[:, c : c + 1], 0.0, FAR)
         x, y, z = (pos[0, n, c : c + 1, :] for n in range(3))
         z = z * HZ
         kind = types[0, c : c + 1, :].astype(F32)
+        near_z.append(z - missing)
         hp[0, :, (1 + c) * N : (2 + c) * N] = jnp.concatenate(
             [x, y, z + missing, kind, jnp.zeros((4, N), F32)], axis=0
         )
-        for n, row in enumerate((x, y, z - missing)):
-            own[c, n] = jnp.broadcast_to(row, (N, N)).T
-    basis = lax.broadcasted_iota(jnp.int32, (K, N), 0).astype(F32)
-    fold = jnp.exp(-0.5 * basis * basis)
-    wk = w_radial[...] * fold
-    for k in range(K):
-        wkt[k] = jnp.broadcast_to(wk[k : k + 1], (N, N)).T
-    for load in loads[4:]:
-        load.wait()
-
-    def slot(kind, place):
+
+    def slot(kind, place, source=False):
         role, column = place
+        if kind == VAL and role == 0 and column in (1, 2) and source:
+            return feat_in.at[0, column - 1]
         if kind == POS:
             return hp.at[role, :, column * N : (column + 1) * N]
         return (hf if kind == VAL else hg).at[role, column * N : (column + 1) * N, :]
@@ -142,7 +136,7 @@
             return
         for src, dst, to, who in messages:
             copy = pltpu.make_async_remote_copy(
-                src_ref=slot(kind, src),
+                src_ref=slot(kind, src, True),
                 dst_ref=slot(kind, dst),
                 send_sem=send_sem.at[len(sent)],
                 recv_sem=recv_sem.at[kind, dst[0] * 4 + dst[1]],
@@ -169,6 +163,17 @@
         pl.semaphore_wait(barrier, len(dev) + 15 + 7)
     send(POS, FIRST)
     send(VAL, FIRST)
+
+    for load in loads[3:]:
+        load.wait()
+    for c in range(2):
+        for n, row in enumerate((pos[0, 0, c : c + 1, :], pos[0, 1, c : c + 1, :], near_z[c])):
+            own[c, n] = jnp.broadcast_to(row, (N, N)).T
+    basis = lax.broadcasted_iota(jnp.int32, (K, N), 0).astype(F32)
+    fold = jnp.exp(-0.5 * basis * basis)
+    wk = w_radial[...] * fold
+    for k in range(K):
+        wkt[k] = jnp.broadcast_to(wk[k : k + 1], (N, N)).T
 
     window = lax.broadcasted_iota(jnp.int32, (1, 3 * N), 1)
     shift_y = (window // N - 1).astype(F32)
@@ -262,31 +267,29 @@
         gather(c, 1, hc, False)
     arrive(VAL, (2, 0), (2, 1), (2, 2), (2, 3))
     values(2)
-    for c in range(2):
-        gather(c, 2, hc, False)
 
     def own_rows(c):
         return slice((1 + c) * N, (2 + c) * N)
 
     pre = []
     halves = []
-    for c in range(2):
+    grad_pre = []
+    sigs = []
+    grad_agg = []
+    for c in range(2):
+        gather(c, 2, hc, False)
         total = usum[c, 0] * wk[0:1]
         for k in range(1, K):
             total = total + usum[c, k] * wk[k : k + 1]
         halves.append(total.astype(BF16))
         pre.append(dot(halves[c], w_out[...]))
-    grad_pre = []
-    sigs = []
-    grad_agg = []
-    for c in range(2):
         sig = jax.nn.sigmoid(pre[c])
         sigs.append(sig)
         grad_pre.append((cot[0, c].astype(F32) * sig * (1.0 + pre[c] * (1.0 - sig))).astype(BF16))
         half = dot(grad_pre[c], w_out[...], ((1,), (1,))).astype(BF16)
         hg[0, own_rows(c), :] = half
         grad_agg.append(half.astype(F32))
-    send(GRAD, FIRST)
+        send(GRAD, [message for message in FIRST if message[0] == (0, 1 + c)])
 
     for c in range(2):
         flipped = grad_agg[c].T
@@ -330,8 +333,7 @@
         )
 
     if COMM:
-        @pl.loop(1, 16)
-        def _(d):
+        for d in range(1, 16):
             q = lax.rem(q_me + d, 16)
             pltpu.make_async_remote_copy(
                 src_ref=ar_src.at[q], dst_ref=ar_one.at[q_me],
@@ -345,8 +347,7 @@
         ar_mid[...] = jnp.sum(ar_one[...].astype(F32), axis=0).astype(BF16)
         ar_two[pl.ds(p_me, 1)] = ar_mid[...][None]
         if COMM:
-            @pl.loop(1, 8)
-            def _(d):
+            for d in range(1, 8):
                 pltpu.make_async_remote_copy(
                     src_ref=ar_mid, dst_ref=ar_two.at[p_me],
                     send_sem=ar_send.at[1], recv_sem=ar_recv.at[1],
@@ -359,8 +360,7 @@
         final = jnp.sum(ar_two[...].astype(F32), axis=0).astype(BF16)
         ar_three[pl.ds(q_me, 1)] = final[None]
         if COMM:
-            @pl.loop(1, 16)
-            def _(d):
+            for d in range(1, 16):
                 pltpu.make_async_remote_copy(
                     src_ref=ar_three.at[q_me], dst_ref=ar_three.at[q_me],
                     send_sem=ar_send.at[2], recv_sem=ar_recv.at[2],
@@ -408,19 +408,19 @@
 
     for c in range(2):
         out_feat[0, c] = (hf[0, own_rows(c), :].astype(F32) + pre[c] * sigs[c]).astype(BF16)
+    middle()
     arrive(GRAD, (0, 0), (0, 3))
     for c in range(2):
         gather(c, 0, hg, True)
-    middle()
+    for c in range(2):
+        pulls(c, 0)
     for col in (1, 2):
         arrive(GRAD, (1, col))
         send(GRAD, RELAY[col])
-    for c in range(2):
-        pulls(c, 0)
+    arrive(GRAD, (1, 0), (1, 3))
+    for c in range(2):
+        gather(c, 1, hg, False)
     collect()
-    arrive(GRAD, (1, 0), (1, 3))
-    for c in range(2):
-        gather(c, 1, hg, False)
     for c in range(2):
         pulls(c, 1)
     arrive(GRAD, (2, 0), (2, 1), (2, 2), (2, 3))
@@ -514,17 +514,20 @@
             pltpu.SemaphoreType.DMA((3,)),
         ],
         compiler_params=pltpu.CompilerParams(
-            collective_id=0, has_side_effects=True, vmem_limit_bytes=60 * 1024 * 1024
+            collective_id=0, has_side_effects=True, vmem_limit_bytes=40 * 1024 * 1024
         ),
         cost_estimate=pl.CostEstimate(flops=4_000_000_000, bytes_accessed=1_000_000, transcendentals=4_000_000),
-    )(features, positions.transpose(0, 2, 1, 3), bead_types, cell_counts, w_value, w_radial, type_gain, w_out, cotangent)
+    )(*(pltpu.with_memory_space_constraint(array, pltpu.HBM) for array in (
+        features, positions.transpose(0, 2, 1, 3), bead_types, cell_counts,
+        w_value, w_radial, type_gain, w_out, cotangent,
+    )))
     out = pl.pallas_call(
         store,
         out_shape=shapes,
         in_specs=[anywhere] * 7,
         out_specs=(pl.BlockSpec(memory_space=pltpu.HBM),) * 7,
         scratch_shapes=[pltpu.SemaphoreType.DMA((7,))],
-        compiler_params=pltpu.CompilerParams(vmem_limit_bytes=60 * 1024 * 1024),
+        compiler_params=pltpu.CompilerParams(vmem_limit_bytes=2 * 1024 * 1024),
     )(*results)
     return (out[0], out[1], out[2].transpose(0, 2, 1, 3)) + tuple(out[3:])
 

time: 67.9 us -> 58.5 us (0.86)
  Pallas kernels: 67.1 us -> 57.7 us
    pallas_call x1, Pallas kernels: 9.57 us -> 0.77 us  [on_device(): pl.pallas_call(store, out_shape=shapes, in_specs=[anywhere] * 7, out_spec...]
where the time goes in v3:
time: 58.5 us; the launch traced here: 58.3 us
  Pallas kernels  57.7 us (99%)
  between operations  0.64 us (1%)
    pallas_call x1, Pallas kernels, on_device(): pl.pallas_call(kernel, out_shape=shapes, in_specs=[pl.BlockSpec(memory_sp...  56.9 us

profile of v3, /device:TPU:1, one launch (start us, length us, event | category | flops | bytes accessed | tf_op | source)
XLA Modules:
  0.0 58.3 jit_solution(14876819159588773548)
XLA Ops:
  0.6 56.9 %shard_map.144 = (bf16[1,2,128,128]{3,2,1,0:T(8,128)(2,1)S(1)}, bf16[1,2,128,128]{3,2,1,0:T(8,128)(2,1)S(1)}, f32[1,3,2,128]{3,2,1,0:T(2,128)S(1)}, f32[128,128]...) custom-call(bf16[1,2,128,128]{3,2,1,0:T(8,128)(2,1)} %feat_in.1, ...), custom_call_target="tpu_custom_call" | custom-call | flops 4000000000 | bytes 1000000 | tf_op jit(solution)/shard_map/pallas_call | solution.py:474
  57.6 0.8 %shard_map.145 = (bf16[1,2,128,128]{3,2,1,0:T(8,128)(2,1)}, bf16[1,2,128,128]{3,2,1,0:T(8,128)(2,1)}, f32[1,3,2,128]{3,2,1,0:T(2,128)}, f32[128,128]{1,0:T(8,128...) custom-call(bf16[1,2,128,128]{3,2,1,0:T(8,128)(2,1)S(1)} %get-tuple-element.21.refs_0_, ...), custom_call_target="tpu_custom_call" | custom-call | tf_op jit(solution)/shard_map/pallas_call | solution.py:524

commit v4 on v3

--- a/solution.py
+++ b/solution.py
@@ -37,6 +37,11 @@
 }
 
 
+EARLY = ((1, 3), (0, 2))
+LATE = ((0, 1), (2, 3))
+ALL = ((0, 3), (0, 3))
+
+
 def dot(a, b, dims=((1,), (0,)), precision=None):
     return lax.dot_general(a, b, (dims, ((), ())), precision=precision, preferred_element_type=F32)
 
@@ -46,7 +51,7 @@
     out_feat, grad_feat, grad_pos, grad_wvalue, grad_wradial, grad_gain, grad_wout,
     hp, hf, hc, hg, own, ebuf, geo, usum, sbuf, lhs, pacc, proj, gain, onehot, wkt, sct, vt,
     pos, types, counts, w_value, w_radial, type_gain, w_out, cot,
-    ar_src, ar_one, ar_mid, ar_two, ar_three,
+    ar_src, ar_one, ar_mid, ar_two, ar_three, ex_one, ex_mid, ex_two, ex_three,
     load_sem, send_sem, recv_sem, ar_send, ar_recv,
 ):
     gx = lax.axis_index("gx")
@@ -65,7 +70,7 @@
         "RW": (other, west), "RE": (other, east),
         "W": (gx, west), "E": (gx, east),
         "P": (beyond, gy), "PW": (beyond, west), "PE": (beyond, east),
-        "Q": (behind, gy), "QW": (behind, west), "QE": (behind, east),
+        "QW": (behind, west), "QE": (behind, east),
     }
     dev = {name: {"gx": x, "gy": y} for name, (x, y) in dev.items()}
     quad = gy // 4
@@ -90,8 +95,13 @@
         load.start()
     barrier = pltpu.get_barrier_semaphore()
     if COMM:
-        for name in dev:
+        for name in ("W", "E", "PW", "PE", "QW", "QE"):
             pl.semaphore_signal(barrier, inc=1, device_id=dev[name], device_id_type=MESH)
+        for edge, names in ((0, ("OW", "RW")), (NY - 1, ("OE", "RE"))):
+            @pl.when(gy == edge)
+            def _():
+                for name in names:
+                    pl.semaphore_signal(barrier, inc=1, device_id=dev[name], device_id_type=MESH)
         for d in range(1, 16):
             pl.semaphore_signal(barrier, inc=1, device_id=group_one(lax.rem(q_me + d, 16)), device_id_type=MESH)
         for d in range(1, 8):
@@ -160,7 +170,15 @@
             ).wait_recv()
 
     if COMM:
-        pl.semaphore_wait(barrier, len(dev) + 15 + 7)
+        at_edge = lax.rem(gy + 1, NY) < 2
+
+        @pl.when(at_edge)
+        def _():
+            pl.semaphore_wait(barrier, 6 + 15 + 7 + 2)
+
+        @pl.when(jnp.logical_not(at_edge))
+        def _():
+            pl.semaphore_wait(barrier, 6 + 15 + 7)
     send(POS, FIRST)
     send(VAL, FIRST)
 
@@ -216,8 +234,12 @@
                 if k < K - 1:
                     value = value * ratio
 
-    def gather(c, role, table, first):
-        got = dot(ebuf[c, role].reshape(K * N, 3 * N), table[role, c * N : (c + 3) * N, :]).reshape(K, N, N)
+    def gather(c, role, table, first, part=ALL):
+        low, high = part[c]
+        got = dot(
+            ebuf[c, role, :, :, low * N : high * N].reshape(K * N, (high - low) * N),
+            table[role, (c + low) * N : (c + high) * N, :],
+        ).reshape(K, N, N)
         if first:
             usum[c] = got
         else:
@@ -230,10 +252,11 @@
         onehot[role] = hot
         gain[role] = dot(hot, type_gain[...], ((0,), (0,)), EXACT)
 
-    def values(role):
-        projected = dot(hf[role], w_value[...])
-        proj[role] = projected
-        hc[role] = (projected * gain[role]).astype(BF16)
+    def values(role, low=0, high=4):
+        span = slice(low * N, high * N)
+        projected = dot(hf[role, span, :], w_value[...])
+        proj[role, span, :] = projected
+        hc[role, span, :] = (projected * gain[role, span, :]).astype(BF16)
 
     arrive(POS, (0, 0), (0, 3))
     for c in range(2):
@@ -261,10 +284,14 @@
     for c in range(2):
         weights(c, 2)
     gains(2)
+    values(1, 1, 3)
+    for c in range(2):
+        gather(c, 1, hc, False, EARLY)
     arrive(VAL, (1, 0), (1, 3))
-    values(1)
-    for c in range(2):
-        gather(c, 1, hc, False)
+    values(1, 0, 1)
+    values(1, 3, 4)
+    for c in range(2):
+        gather(c, 1, hc, False, LATE)
     arrive(VAL, (2, 0), (2, 1), (2, 2), (2, 3))
     values(2)
 
@@ -314,15 +341,9 @@
 
     for q in range(16):
         own_q = slice(8 * q, 8 * q + 8)
-        ar_src[q] = jnp.concatenate(
-            [
-                value_part[own_q],
-                wout_part[own_q],
-                jnp.broadcast_to(gain_part[q : q + 1], (8, N)),
-                jnp.broadcast_to(wradial_part[q % K : q % K + 1], (8, N)),
-            ],
-            axis=0,
-        ).astype(BF16)
+        ar_src[q] = jnp.concatenate([value_part[own_q], wout_part[own_q]], axis=0).astype(BF16)
+    ar_src[16] = gain_part.astype(BF16)
+    ar_src[17] = jnp.concatenate([wradial_part, wradial_part], axis=0).astype(BF16)
     ar_one[pl.ds(q_me, 1)] = ar_src[pl.ds(q_me, 1)]
 
     def batch(buffer, count, phase):
@@ -340,6 +361,28 @@
                 send_sem=ar_send.at[0], recv_sem=ar_recv.at[0],
                 device_id=group_one(q), device_id_type=MESH,
             ).start()
+
+    def extra(j):
+        return pltpu.make_async_remote_copy(
+            src_ref=ar_src.at[16 + j], dst_ref=ex_one.at[q_me],
+            send_sem=ar_send.at[3 + j], recv_sem=ar_recv.at[3],
+            device_id=group_one(j), device_id_type=MESH,
+        )
+
+    def extra_final(j):
+        return pltpu.make_async_remote_copy(
+            src_ref=ex_three.at[j], dst_ref=ex_three.at[j],
+            send_sem=ar_send.at[6], recv_sem=ar_recv.at[5 + j],
+            device_id=dev["W"], device_id_type=MESH,
+        )
+
+    for j in range(2):
+        @pl.when(q_me == j)
+        def _():
+            ex_one[pl.ds(j, 1)] = ar_src[pl.ds(16 + j, 1)]
+
+        if COMM:
+            pl.when(q_me != j)(extra(j).start)
 
     def middle():
         if COMM:
@@ -354,6 +397,18 @@
                     device_id=group_two(lax.rem(p_me + d, 8)), device_id_type=MESH,
                 ).start()
 
+            @pl.when(q_me < 2)
+            def _():
+                batch(ex_one, 15, 3).wait_recv()
+                ex_mid[...] = jnp.sum(ex_one[...].astype(F32), axis=0).astype(BF16)
+                ex_two[pl.ds(p_me, 1)] = ex_mid[...][None]
+                for d in range(1, 8):
+                    pltpu.make_async_remote_copy(
+                        src_ref=ex_mid, dst_ref=ex_two.at[p_me],
+                        send_sem=ar_send.at[5], recv_sem=ar_recv.at[4],
+                        device_id=group_two(lax.rem(p_me + d, 8)), device_id_type=MESH,
+                    ).start()
+
     def collect():
         if COMM:
             batch(ar_two, 7, 1).wait_recv()
@@ -367,62 +422,90 @@
                     device_id=group_one(lax.rem(q_me + d, 16)), device_id_type=MESH,
                 ).start()
 
+            for j in range(2):
+                @pl.when(q_me == j)
+                def _():
+                    batch(ex_two, 7, 4).wait_recv()
+                    ex_three[j] = jnp.sum(ex_two[...].astype(F32), axis=0).astype(BF16)
+                    for d in range(1, 16):
+                        pltpu.make_async_remote_copy(
+                            src_ref=ex_three.at[j], dst_ref=ex_three.at[j],
+                            send_sem=ar_send.at[6], recv_sem=ar_recv.at[5 + j],
+                            device_id=group_one((j + d) % 16), device_id_type=MESH,
+                        ).start()
+
     def finish():
         if COMM:
             batch(ar_three, 15, 2).wait_recv()
+            for j in range(2):
+                pl.when(q_me != j)(extra_final(j).wait_recv)
         for q in range(16):
             chunk = ar_three[q].astype(F32)
             grad_wvalue[8 * q : 8 * q + 8, :] = chunk[0:8]
             grad_wout[8 * q : 8 * q + 8, :] = chunk[8:16]
-            grad_gain[q : q + 1, :] = chunk[16:17]
-            if q < K:
-                grad_wradial[q : q + 1, :] = chunk[24:25]
+        grad_gain[...] = ex_three[0].astype(F32)
+        grad_wradial[...] = ex_three[1].astype(F32)[:K]
 
     for c in range(2):
         for k in range(K):
             lhs[c, k, :, :N] = (grad_agg[c] * wk[k : k + 1]).astype(BF16)
         pacc[c] = jnp.zeros((3, N, N), F32)
 
-    def pulls(c, role):
-        span = slice(c * N, (c + 3) * N)
+    def pulls(c, role, part=ALL):
+        low, high = part[c]
+        wide = high - low
+        rows = 64 // wide if wide < 3 else ROWS
+        span = slice((c + low) * N, (c + high) * N)
+        lanes = slice(low * N, high * N)
         both = jnp.concatenate([hc[role, span, :], hg[role, span, :]], axis=1)
-        sbuf[...] = dot(lhs[c].reshape(K * N, 2 * N), both, ((1,), (1,))).reshape(K, N, 3 * N)
-        near_rows = near(c, role)
-
-        @pl.loop(0, N // ROWS)
+        sbuf[:, :, : wide * N] = dot(lhs[c].reshape(K * N, 2 * N), both, ((1,), (1,))).reshape(K, N, wide * N)
+        near_rows = [row[:, lanes] for row in near(c, role)]
+
+        @pl.loop(0, N // rows)
         def _(i):
-            i0 = pl.multiple_of(i * ROWS, ROWS)
-            deltas = deltas_of(c, near_rows, i0)
-            ratio = geo[c, role, 0, pl.ds(i0, ROWS), :]
-            total = sbuf[K - 1, pl.ds(i0, ROWS), :]
+            some = pl.ds(pl.multiple_of(i * rows, rows), rows)
+            ratio = geo[c, role, 0, some, lanes]
+            total = sbuf[K - 1, some, : wide * N]
             slope = total
             for k in range(K - 2, -1, -1):
-                total = total * ratio + sbuf[k, pl.ds(i0, ROWS), :]
+                total = total * ratio + sbuf[k, some, : wide * N]
                 if k > 0:
                     slope = slope * ratio + total
             slope = slope * ratio
-            pull = geo[c, role, 1, pl.ds(i0, ROWS), :] * total - geo[c, role, 2, pl.ds(i0, ROWS), :] * slope
+            pull = geo[c, role, 1, some, lanes] * total - geo[c, role, 2, some, lanes] * slope
             for n in range(3):
-                part = pull * deltas[n]
-                pacc[c, n, pl.ds(i0, ROWS), :] += part[:, :N] + part[:, N : 2 * N] + part[:, 2 * N :]
+                mine = own[c, n, some, :]
+                moved = pacc[c, n, some, :]
+                for w in range(wide):
+                    block = slice(w * N, (w + 1) * N)
+                    moved = moved + pull[:, block] * (near_rows[n][:, block] - mine)
+                pacc[c, n, some, :] = moved
 
     for c in range(2):
         out_feat[0, c] = (hf[0, own_rows(c), :].astype(F32) + pre[c] * sigs[c]).astype(BF16)
+    for c in range(2):
+        gather(c, 0, hg, True, EARLY)
+    for c in range(2):
+        pulls(c, 0, EARLY)
     middle()
     arrive(GRAD, (0, 0), (0, 3))
     for c in range(2):
-        gather(c, 0, hg, True)
-    for c in range(2):
-        pulls(c, 0)
+        gather(c, 0, hg, False, LATE)
+    for c in range(2):
+        pulls(c, 0, LATE)
     for col in (1, 2):
         arrive(GRAD, (1, col))
         send(GRAD, RELAY[col])
+    for c in range(2):
+        gather(c, 1, hg, False, EARLY)
+    for c in range(2):
+        pulls(c, 1, EARLY)
+    collect()
     arrive(GRAD, (1, 0), (1, 3))
     for c in range(2):
-        gather(c, 1, hg, False)
-    collect()
-    for c in range(2):
-        pulls(c, 1)
+        gather(c, 1, hg, False, LATE)
+    for c in range(2):
+        pulls(c, 1, LATE)
     arrive(GRAD, (2, 0), (2, 1), (2, 2), (2, 3))
     for c in range(2):
         gather(c, 2, hg, False)
@@ -446,6 +529,19 @@
         batch(ar_one, 15, 0).wait_send()
         batch(ar_two, 7, 1).wait_send()
         batch(ar_three, 15, 2).wait_send()
+        for j in range(2):
+            pl.when(q_me != j)(extra(j).wait_send)
+
+        @pl.when(q_me < 2)
+        def _():
+            pltpu.make_async_remote_copy(
+                src_ref=ex_two.at[pl.ds(0, 7)], dst_ref=ex_two.at[pl.ds(0, 7)],
+                send_sem=ar_send.at[5], recv_sem=ar_recv.at[4], device_id=dev["W"], device_id_type=MESH,
+            ).wait_send()
+            pltpu.make_async_remote_copy(
+                src_ref=ex_one.at[pl.ds(0, 15)], dst_ref=ex_one.at[pl.ds(0, 15)],
+                send_sem=ar_send.at[6], recv_sem=ar_recv.at[3], device_id=dev["W"], device_id_type=MESH,
+            ).wait_send()
 
 
 def store(*refs):
@@ -502,16 +598,20 @@
             pltpu.VMEM((16, N), F32),
             pltpu.VMEM((N, N), BF16),
             pltpu.VMEM((1, 2, N, N), BF16),
-            pltpu.VMEM((16, 32, N), BF16),
-            pltpu.VMEM((16, 32, N), BF16),
-            pltpu.VMEM((32, N), BF16),
-            pltpu.VMEM((8, 32, N), BF16),
-            pltpu.VMEM((16, 32, N), BF16),
+            pltpu.VMEM((18, 16, N), BF16),
+            pltpu.VMEM((16, 16, N), BF16),
+            pltpu.VMEM((16, N), BF16),
+            pltpu.VMEM((8, 16, N), BF16),
+            pltpu.VMEM((16, 16, N), BF16),
+            pltpu.VMEM((16, 16, N), BF16),
+            pltpu.VMEM((16, N), BF16),
+            pltpu.VMEM((8, 16, N), BF16),
+            pltpu.VMEM((2, 16, N), BF16),
             pltpu.SemaphoreType.DMA((10,)),
             pltpu.SemaphoreType.DMA((42,)),
             pltpu.SemaphoreType.DMA((3, 12)),
-            pltpu.SemaphoreType.DMA((3,)),
-            pltpu.SemaphoreType.DMA((3,)),
+            pltpu.SemaphoreType.DMA((7,)),
+            pltpu.SemaphoreType.DMA((7,)),
         ],
         compiler_params=pltpu.CompilerParams(
             collective_id=0, has_side_effects=True, vmem_limit_bytes=40 * 1024 * 1024

time: 58.5 us -> 56.2 us (0.961)
  Pallas kernels: 57.7 us -> 55.4 us
    pallas_call x1, Pallas kernels: 56.9 us -> 54.6 us  [on_device(): pl.pallas_call(kernel, out_shape=shapes, in_specs=[pl.BlockSpec(memory_sp...]
where the time goes in v4:
time: 56.2 us; the launch traced here: 56 us
  Pallas kernels  55.4 us (99%)
  between operations  0.64 us (1%)
    pallas_call x1, Pallas kernels, on_device(): pl.pallas_call(kernel, out_shape=shapes, in_specs=[pl.BlockSpec(memory_sp...  54.6 us

profile of v4, /device:TPU:1, one launch (start us, length us, event | category | flops | bytes accessed | tf_op | source)
XLA Modules:
  0.0 56.0 jit_solution(14924737602496783979)
XLA Ops:
  0.6 54.6 %shard_map.144 = (bf16[1,2,128,128]{3,2,1,0:T(8,128)(2,1)S(1)}, bf16[1,2,128,128]{3,2,1,0:T(8,128)(2,1)S(1)}, f32[1,3,2,128]{3,2,1,0:T(2,128)S(1)}, f32[128,128]...) custom-call(bf16[1,2,128,128]{3,2,1,0:T(8,128)(2,1)} %feat_in.1, ...), custom_call_target="tpu_custom_call" | custom-call | flops 4000000000 | bytes 1000000 | tf_op jit(solution)/shard_map/pallas_call | solution.py:570
  55.2 0.8 %shard_map.145 = (bf16[1,2,128,128]{3,2,1,0:T(8,128)(2,1)}, bf16[1,2,128,128]{3,2,1,0:T(8,128)(2,1)}, f32[1,3,2,128]{3,2,1,0:T(2,128)}, f32[128,128]{1,0:T(8,128...) custom-call(bf16[1,2,128,128]{3,2,1,0:T(8,128)(2,1)S(1)} %get-tuple-element.21.refs_0_, ...), custom_call_target="tpu_custom_call" | custom-call | tf_op jit(solution)/shard_map/pallas_call | solution.py:624

commit v5 on v4

--- a/solution.py
+++ b/solution.py
@@ -32,8 +32,8 @@
     ((0, 2), (2, 0), "RE", "last"),
 )
 RELAY = {
-    1: (((1, 1), (2, 1), "P", "all"), ((1, 1), (1, 3), "W", "not first"), ((1, 1), (2, 3), "PW", "not first")),
-    2: (((1, 2), (2, 2), "P", "all"), ((1, 2), (1, 0), "E", "not last"), ((1, 2), (2, 0), "PE", "not last")),
+    1: (((1, 1), (2, 3), "PW", "not first"), ((1, 1), (2, 1), "P", "all"), ((1, 1), (1, 3), "W", "not first")),
+    2: (((1, 2), (2, 0), "PE", "not last"), ((1, 2), (2, 2), "P", "all"), ((1, 2), (1, 0), "E", "not last")),
 }
 
 
@@ -298,6 +298,7 @@
     def own_rows(c):
         return slice((1 + c) * N, (2 + c) * N)
 
+    early_sent = len(sent)
     pre = []
     halves = []
     grad_pre = []
@@ -332,7 +333,11 @@
         given = vt[role].T
         half = (given * gain[role]).astype(BF16)
         value_part = value_part + dot(hf[role], half, ((0,), (0,)))
-        gain_part = gain_part + dot(onehot[role], given * proj[role], precision=EXACT)
+        product = given * proj[role]
+        upper = product.astype(BF16)
+        lower = (product - upper.astype(F32)).astype(BF16)
+        both = dot(onehot[role].astype(BF16), jnp.concatenate([upper, lower], axis=1))
+        gain_part = gain_part + (both[:, :N] + both[:, N:])
     wout_part = dot(halves[0], grad_pre[0], ((0,), (0,))) + dot(halves[1], grad_pre[1], ((0,), (0,)))
     rows = []
     for k in range(K):
@@ -487,6 +492,9 @@
         gather(c, 0, hg, True, EARLY)
     for c in range(2):
         pulls(c, 0, EARLY)
+    if COMM:
+        for who, copy in sent[:early_sent]:
+            where_sent(who, copy.wait_send)
     middle()
     arrive(GRAD, (0, 0), (0, 3))
     for c in range(2):
@@ -522,12 +530,13 @@
         for n in range(3):
             scale = 2.0 * (HZ if n == 2 else 1.0)
             grad_pos[0, n, c : c + 1, :] = jnp.sum(pacc[c, n].T, axis=0, keepdims=True) * scale
-    finish()
     if COMM:
-        for who, copy in sent:
+        for who, copy in sent[early_sent:]:
             where_sent(who, copy.wait_send)
         batch(ar_one, 15, 0).wait_send()
         batch(ar_two, 7, 1).wait_send()
+    finish()
+    if COMM:
         batch(ar_three, 15, 2).wait_send()
         for j in range(2):
             pl.when(q_me != j)(extra(j).wait_send)

time: 56.2 us -> 56 us (level)
  no operation moved by 1% of the time
where the time goes in v5:
time: 56 us; the launch traced here: 55.9 us
  Pallas kernels  55.3 us (99%)
  between operations  0.64 us (1%)
    pallas_call x1, Pallas kernels, on_device(): pl.pallas_call(kernel, out_shape=shapes, in_specs=[pl.BlockSpec(memory_sp...  54.5 us

profile of v5, /device:TPU:1, one launch (start us, length us, event | category | flops | bytes accessed | tf_op | source)
XLA Modules:
  0.0 55.9 jit_solution(39702548778037274)
XLA Ops:
  0.6 54.5 %shard_map.144 = (bf16[1,2,128,128]{3,2,1,0:T(8,128)(2,1)S(1)}, bf16[1,2,128,128]{3,2,1,0:T(8,128)(2,1)S(1)}, f32[1,3,2,128]{3,2,1,0:T(2,128)S(1)}, f32[128,128]...) custom-call(bf16[1,2,128,128]{3,2,1,0:T(8,128)(2,1)} %feat_in.1, ...), custom_call_target="tpu_custom_call" | custom-call | flops 4000000000 | bytes 1000000 | tf_op jit(solution)/shard_map/pallas_call | solution.py:579
  55.1 0.8 %shard_map.145 = (bf16[1,2,128,128]{3,2,1,0:T(8,128)(2,1)}, bf16[1,2,128,128]{3,2,1,0:T(8,128)(2,1)}, f32[1,3,2,128]{3,2,1,0:T(2,128)}, f32[128,128]{1,0:T(8,128...) custom-call(bf16[1,2,128,128]{3,2,1,0:T(8,128)(2,1)S(1)} %get-tuple-element.21.refs_0_, ...), custom_call_target="tpu_custom_call" | custom-call | tf_op jit(solution)/shard_map/pallas_call | solution.py:633
